TPU v7x, 128 devices: a whole 4x4x4 slice. The times are simulated.
128 devices in a mesh: row: 8 (over z, core), col: 16 (over x, y).
Axes of the slice: x: 4, y: 4, z: 4, core: 2. Of those that a mesh axis runs over, the one named last changes fastest.
Arguments:
- object_slices: float32 [2, 2, 4096, 4096], P(None, None, 'row', 'col'), may hold values from -6 to 6
- probe: bfloat16 [4, 2, 256, 256], replicated, may hold values from -6 to 6
- measured: float32 [768, 256, 256], P(('row', 'col')), may hold values from 0 to 3
- tap_row: float32 [2, 64], replicated, may hold values from -0.5 to 0.5
- tap_col: float32 [2, 64], replicated, may hold values from -0.5 to 0.5
- scan_corner: int32 [768, 2], P(('row', 'col')), may hold values from 0 to 3840, as said below
- correlation: int32 [768, 2], P(('row', 'col')), may hold values from 0 to 15, as said below
- scan_count: int32 [8, 16], P('row', 'col'), may hold values from 1 to 6, as said below
Outputs:
- object_grad: float32 [2, 2, 4096, 4096], P(None, None, 'row', 'col')
- probe_grad: float32 [4, 2, 256, 256], replicated
Inputs may be any that keep to these rules, and one draw needn't show every extreme that they name: `scan_corner`: the scans of the device at mesh row r start at pixel row r * 512 + a * 128 with a one of 0, 1, 2, and at a pixel column that is a multiple of 128; the left half of the patch lies in tile column correlation[n, 0] and the right half in correlation[n, 1]. correlation[n, 1] equals correlation[n, 0] or is one more. From one device at most 2 patch halves fall in one tile column; in every draw each mesh row has a tile column that receives 2 halves from every device of that row. `scan_count`: slots of a device below its count are live; some device has all 6 live.
All inputs are finite; a program needn't handle non-finite values.
Results may differ from a plain program's by a relative error of at most 0.009.
The roundings to bfloat16 on the way count: a program that leaves them out, or rounds other values in their place, can miss the bound.
Values may be sent and summed in bfloat16 or wider, within the bound.
No kernel may reach another device: no remote copies, remote signals or barrier semaphores. Data moves between devices by JAX's collectives and lax.ppermute only.
A program may use at most 128 MiB of HBM per device.

v0:
```python
import math

import jax
import jax.numpy as jnp
import numpy as np
from jax import lax
from jax.experimental import pallas as pl
from jax.experimental.pallas import tpu as pltpu
from jax.sharding import PartitionSpec as P

SIZE = 256
HALF = 128
MODES = 4
CHUNK = 32
SLOTS = 8
BF16 = jnp.bfloat16
F32 = jnp.float32


def dft_tables():
    index = np.arange(SIZE)
    phase = 2.0 * np.pi * ((index[:, None] * index[None, :]) % SIZE) / SIZE
    real = np.cos(phase) / math.sqrt(SIZE)
    imag = -np.sin(phase) / math.sqrt(SIZE)
    left = np.block([[real, -imag], [imag, real]])
    right = np.block([[real, imag], [-imag, real]])
    return jnp.asarray(left, F32).astype(BF16), jnp.asarray(right, F32).astype(BF16)


def describe_kernel(info, notes):
    tiles = notes.shape[0] // SLOTS
    scans = (info.shape[0] - 2) // 4
    level = [(info[2 * n] // HALF) % 4 for n in range(scans)]
    straddles = [(info[2 * n + 1] // HALF) % 2 for n in range(scans)]
    tile = [info[2 * scans + 2 * n] for n in range(scans)]
    live = [(n < info[4 * scans]).astype(jnp.int32) for n in range(scans)]
    zero = jnp.int32(0)
    before, after = [zero] * scans, [zero] * scans
    for two in range(scans):
        for one in range(two):
            same = (tile[one] == tile[two]) & (straddles[one] + straddles[two] == 2)
            same = same.astype(jnp.int32)
            before[two], after[one] = before[two] | same, after[one] | same
    owner = [tile[n] + before[n] for n in range(scans)]
    odd = info[4 * scans + 1]
    aside = 2 * odd - 1
    other = [
        lax.rem(tile[n] + straddles[n] + (1 - straddles[n]) * aside + tiles, tiles)
        for n in range(scans)
    ]
    for n in range(scans):
        free = live[n] * (1 - before[n]) * (1 - after[n])
        for k in range(scans):
            if k != n:
                free = free * (1 - (owner[k] == other[n]).astype(jnp.int32))
            if k < n:
                free = free * (1 - (other[k] == other[n]).astype(jnp.int32))
        column = (1 + straddles[n] - 2 * before[n] + odd) & 3
        moved_column = (3 * (1 - straddles[n]) + odd) & 3
        note = live[n] + 2 * free + 4 * owner[n] + 64 * other[n] + 1024 * level[n]
        note = note + 4096 * column + 16384 * moved_column
        for t in range(tiles):
            notes[t * SLOTS + n] = note
    for t in range(tiles):
        for n in range(scans, SLOTS):
            notes[t * SLOTS + n] = 0


def assign_kernel(me, notes, codes, homes, loads, moves):
    tiles = codes.shape[0]
    scans = homes.shape[0]
    for t in range(tiles):
        loads[t] = 0
        codes[t] = 0

    def fields(place):
        note = notes[place]
        return note & 1, (note >> 1) & 1, (note >> 2) & 15, (note >> 6) & 15, note

    @pl.loop(0, tiles)
    def _(source):
        for n in range(scans):
            live, _, owner, _, _ = fields(source * SLOTS + n)
            loads[owner] += live
            moves[source * SLOTS + n] = 0

    for _ in range(2):

        @pl.loop(0, tiles)
        def _(source):
            for n in range(scans):
                place = source * SLOTS + n
                _, free, owner, other, _ = fields(place)
                gain = (loads[owner] > loads[other] + 1).astype(jnp.int32)
                step = free * gain * (1 - moves[place])
                loads[owner] -= step
                loads[other] += step
                moves[place] += step

    @pl.loop(0, tiles)
    def _(source):
        code = jnp.int32(0)
        for n in range(scans):
            place = source * SLOTS + n
            live, _, owner, other, note = fields(place)
            moved = moves[place] == 1
            home = jnp.where(moved, other, owner)
            column = jnp.where(moved, (note >> 14) & 3, (note >> 12) & 3)
            here = live * (home == me[0]).astype(jnp.int32)
            code = code + here * (1 + 4 * ((note >> 10) & 3) + column)

            @pl.when(source == me[0])
            def _():
                homes[n] = jnp.where(live == 1, home, -1)

        codes[source] = code


def cast_kernel(odd, obj, tile_low, half):
    side = pl.multiple_of((1 - odd[0]) * HALF, HALF)
    tile_low[...] = obj[...].astype(BF16)
    half[...] = obj[:, :, :, pl.ds(side, HALF)].astype(BF16)


def pack_kernel(homes, measured, slots):
    for n in range(measured.shape[0]):

        @pl.when(homes[n] >= 0)
        def _():
            slots[homes[n]] = measured[n].astype(BF16)


def table_kernel(taps, tables, adjoints):
    def banded(row, shift):
        line = jnp.broadcast_to(taps[row : row + 1, :], (SIZE, 2 * SIZE))
        return pltpu.roll(line, shift, 1, stride=1, stride_axis=0)[:, :SIZE]

    straight, turned = 2 * SIZE - 32, 2 * SIZE - 31

    def put(out, real, imag, from_left):
        sign = 1.0 if from_left else -1.0
        out[:SIZE, :SIZE] = real.astype(BF16)
        out[:SIZE, SIZE:] = (-sign * imag).astype(BF16)
        out[SIZE:, :SIZE] = (sign * imag).astype(BF16)
        out[SIZE:, SIZE:] = real.astype(BF16)

    put(tables.at[0], banded(0, straight), banded(1, straight), True)
    put(tables.at[1], banded(6, turned), banded(7, turned), False)
    put(adjoints.at[0], banded(4, turned), -banded(5, turned), True)
    put(adjoints.at[1], banded(2, straight), -banded(3, straight), False)


CHUNKS = [slice(at, at + CHUNK) for at in range(0, SIZE, CHUNK)]


def left_stage(table, rows_in, cols_in):
    for m in range(MODES):
        both = jnp.dot(table, rows_in[m], preferred_element_type=F32)
        here = slice(m * SIZE, (m + 1) * SIZE)
        cols_in[here, :SIZE] = both[:SIZE].astype(BF16)
        cols_in[here, SIZE:] = both[SIZE:].astype(BF16)


def right_stage(table, cols_in, out):
    for m in range(MODES):
        here = slice(m * SIZE, (m + 1) * SIZE)
        out[here, :] = jnp.dot(cols_in[here, :], table, preferred_element_type=F32)


def put_rows(rows_in, m, at, real, imag):
    rows_in[m, at.start : at.stop, :] = real.astype(BF16)
    rows_in[m, SIZE + at.start : SIZE + at.stop, :] = imag.astype(BF16)


def pair(ref, m, at):
    here = slice(m * SIZE + at.start, m * SIZE + at.stop)
    return ref[here, :SIZE], ref[here, SIZE:]


def extend(odd, full, tile, half, ext):
    ext[4 * odd] = half[...]
    ext[1 + odd], ext[2 + odd] = tile[:, :, :, :HALF], tile[:, :, :, HALF:]
    ext[3 - 3 * odd], ext[4 - 3 * odd] = full[:, :, :, :HALF], full[:, :, :, HALF:]


def live_list(codes, order):
    def note(slot, found):
        live = codes[slot] > 0

        @pl.when(live)
        def _():
            order[found] = slot

        return found + live.astype(jnp.int32)

    return lax.fori_loop(0, codes.shape[0], note, jnp.int32(0))


def place_of(code):
    return (code - 1) % 4, pl.multiple_of(((code - 1) // 4) * HALF, HALF)


def pair_of(patch, s, at):
    return patch[s, at, :SIZE].astype(F32), patch[s, at, SIZE:].astype(F32)


def forward_kernel(
    odd, codes, full, tile, half, probe, tables, dft_left, dft_right,
    moved_all, far_all, root_all, patch_all,
    ext, rows_in, cols_in, moved_two, far_two, root_two, patch_two, order, sems,
):
    extend(odd[0], full, tile, half, ext)
    found = live_list(codes, order)
    wholes = (moved_all, far_all, root_all, patch_all)
    buffers = (moved_two, far_two, root_two, patch_two)

    def copies(i):
        two = lax.rem(i, 2)
        return [
            pltpu.make_async_copy(buffers[k].at[two], wholes[k].at[order[i]], sems.at[two, k])
            for k in range(4)
        ]

    @pl.loop(0, found)
    def _(i):
        two = lax.rem(i, 2)
        moved, far, root, patch = (buffer.at[two] for buffer in buffers)

        @pl.when(i >= 2)
        def _():
            for copy in copies(i - 2):
                copy.wait()

        column, start = place_of(codes[order[i]])
        for s in range(2):
            for part in range(2):
                for side in range(2):
                    low = part * SIZE + side * HALF
                    patch[s, :, low : low + HALF] = ext[column + side, s, part, pl.ds(start, SIZE), :]
        for at in CHUNKS:
            o_re, o_im = pair_of(patch, 0, at)
            for m in range(MODES):
                p_re, p_im = probe[m, 0, at, :].astype(F32), probe[m, 1, at, :].astype(F32)
                put_rows(rows_in, m, at, p_re * o_re - p_im * o_im, p_re * o_im + p_im * o_re)
        left_stage(tables[0], rows_in, cols_in)
        right_stage(tables[1], cols_in, moved)
        for at in CHUNKS:
            o_re, o_im = pair_of(patch, 1, at)
            for m in range(MODES):
                v_re, v_im = pair(moved, m, at)
                put_rows(rows_in, m, at, v_re * o_re - v_im * o_im, v_re * o_im + v_im * o_re)
        left_stage(dft_left[...], rows_in, cols_in)
        right_stage(dft_right[...], cols_in, far)
        for at in CHUNKS:
            power = jnp.ones((CHUNK, SIZE), F32)
            for m in range(MODES):
                f_re, f_im = pair(far, m, at)
                power = power + (f_re * f_re + f_im * f_im)
            root[at, :] = 1.0 / jnp.sqrt(power)
        for copy in copies(i):
            copy.start()

    for last in (2, 1):

        @pl.when(found >= last)
        def _():
            for copy in copies(found - last):
                copy.wait()


def backward_kernel(
    odd, codes, dft_left, dft_right, probe_all, adjoints_all,
    moved_all, far_all, root_all, patch_all, slots_all,
    own_grad, full_grad, half_grad, probe_grad,
    rows_in, cols_in, moved_two, far_two, root_two, patch_two, slots_two,
    probe, adjoints, acc, probe_acc, order, sems, once, ends,
):
    found = live_list(codes, order)
    wholes = (far_all, slots_all, root_all, moved_all, patch_all)
    buffers = (far_two, slots_two, root_two, moved_two, patch_two)
    tables = [
        pltpu.make_async_copy(probe_all, probe, once.at[0]),
        pltpu.make_async_copy(adjoints_all, adjoints, once.at[1]),
    ]

    def copies(i):
        two = lax.rem(i, 2)
        return [
            pltpu.make_async_copy(wholes[k].at[order[i]], buffers[k].at[two], sems.at[two, k])
            for k in range(5)
        ]

    @pl.when(found > 0)
    def _():
        for copy in copies(0) + tables:
            copy.start()

    acc[...] = jnp.zeros(acc.shape, F32)
    probe_acc[...] = jnp.zeros(probe_acc.shape, F32)

    def add_piece(s, at, column, start, g_re, g_im):
        rows = pl.ds(pl.multiple_of(start + at.start, CHUNK), CHUNK)
        for part, value in ((0, g_re), (1, g_im)):
            value = value.astype(BF16).astype(F32)
            for side in range(2):
                acc[column + side, s, part, rows, :] += value[:, side * HALF : (side + 1) * HALF]

    @pl.loop(0, found)
    def _(i):
        two = lax.rem(i, 2)
        far, slot, root, moved, patch = (buffer.at[two] for buffer in buffers)

        @pl.when(i + 1 < found)
        def _():
            for copy in copies(i + 1):
                copy.start()

        column, start = place_of(codes[order[i]])
        for copy in copies(i):
            copy.wait()
        for at in CHUNKS:
            factor = 1.0 - slot[at, :].astype(F32) * root[at, :]
            for m in range(MODES):
                f_re, f_im = pair(far, m, at)
                put_rows(rows_in, m, at, factor * f_re, factor * f_im)
        left_stage(dft_right[...], rows_in, cols_in)
        right_stage(dft_left[...], cols_in, far)
        for at in CHUNKS:
            o_re, o_im = pair_of(patch, 1, at)
            g_re = jnp.zeros((CHUNK, SIZE), F32)
            g_im = jnp.zeros((CHUNK, SIZE), F32)
            for m in range(MODES):
                a_re, a_im = pair(far, m, at)
                v_re, v_im = pair(moved, m, at)
                g_re = g_re + (v_re * a_re + v_im * a_im)
                g_im = g_im + (v_re * a_im - v_im * a_re)
                put_rows(rows_in, m, at, o_re * a_re + o_im * a_im, o_re * a_im - o_im * a_re)
            add_piece(1, at, column, start, g_re, g_im)

        @pl.when(i == 0)
        def _():
            for copy in tables:
                copy.wait()

        left_stage(adjoints[0], rows_in, cols_in)
        right_stage(adjoints[1], cols_in, moved)
        for at in CHUNKS:
            o_re, o_im = pair_of(patch, 0, at)
            g_re = jnp.zeros((CHUNK, SIZE), F32)
            g_im = jnp.zeros((CHUNK, SIZE), F32)
            for m in range(MODES):
                i_re, i_im = pair(moved, m, at)
                p_re, p_im = probe[m, 0, at, :].astype(F32), probe[m, 1, at, :].astype(F32)
                g_re = g_re + (p_re * i_re + p_im * i_im)
                g_im = g_im + (p_re * i_im - p_im * i_re)
                probe_acc[m, 0, at, :] += o_re * i_re + o_im * i_im
                probe_acc[m, 1, at, :] += o_re * i_im - o_im * i_re
            add_piece(0, at, column, start, g_re, g_im)

    leave = [
        pltpu.make_async_copy(
            acc.at[1 + side + odd[0]],
            own_grad.at[:, :, :, pl.ds(side * HALF, HALF)],
            ends.at[side],
        )
        for side in range(2)
    ]
    for copy in leave:
        copy.start()
    half_grad[...] = acc[4 * odd[0]].astype(BF16)
    full_grad[:, :, :, :HALF] = acc[3 - 3 * odd[0]].astype(BF16)
    full_grad[:, :, :, HALF:] = acc[4 - 3 * odd[0]].astype(BF16)
    probe_grad[...] = probe_acc[...].astype(BF16)
    for copy in leave:
        copy.wait()


def whole(count):
    return [pl.BlockSpec(memory_space=pltpu.VMEM) for _ in range(count)]


def scalars(count):
    return [pl.BlockSpec(memory_space=pltpu.SMEM) for _ in range(count)]


def body(object_slices, probe, measured, tap_row, tap_col, scan_corner, correlation, scan_count):
    cols = lax.axis_size("col")
    rows = lax.axis_size("row")
    band = object_slices.shape[2]
    part_shape = (2, 2, band, HALF)
    limit = pltpu.CompilerParams(vmem_limit_bytes=56 * 1024 * 1024)

    tile_shape = (2, 2, band, SIZE)
    scans = measured.shape[0]
    odd = (lax.axis_index("row") % 2).reshape(1)
    info = [scan_corner.reshape(-1), correlation.reshape(-1), scan_count.reshape(-1), odd]
    notes = pl.pallas_call(
        describe_kernel,
        out_shape=jax.ShapeDtypeStruct((cols * SLOTS,), jnp.int32),
        in_specs=scalars(1),
        out_specs=pl.BlockSpec(memory_space=pltpu.SMEM),
        compiler_params=limit,
    )(jnp.concatenate(info))
    notes, object_slices = lax.optimization_barrier((notes, object_slices))
    row_notes = lax.all_to_all(
        notes.reshape(cols, SLOTS), "col", split_axis=0, concat_axis=0, tiled=True
    )
    tile_low, half = pl.pallas_call(
        cast_kernel,
        out_shape=[
            jax.ShapeDtypeStruct(tile_shape, BF16),
            jax.ShapeDtypeStruct(part_shape, BF16),
        ],
        in_specs=scalars(1) + whole(1),
        out_specs=whole(2),
        compiler_params=limit,
    )(odd, object_slices)
    row_notes, tile_low, half = lax.optimization_barrier((row_notes, tile_low, half))

    def ring(step):
        pairs = []
        for r in range(rows):
            way = step if r % 2 == 0 else -step
            pairs += [(r * cols + c, r * cols + (c + way) % cols) for c in range(cols)]
        return pairs

    both = ("row", "col")
    full = lax.ppermute(tile_low, both, ring(-1))
    half = lax.ppermute(half, both, ring(1))
    codes, homes = pl.pallas_call(
        assign_kernel,
        out_shape=[
            jax.ShapeDtypeStruct((cols,), jnp.int32),
            jax.ShapeDtypeStruct((scans,), jnp.int32),
        ],
        in_specs=scalars(2),
        out_specs=scalars(2),
        scratch_shapes=[
            pltpu.SMEM((cols,), jnp.int32),
            pltpu.SMEM((cols * SLOTS,), jnp.int32),
        ],
        compiler_params=limit,
    )(lax.axis_index("col").reshape(1), row_notes.reshape(cols * SLOTS))
    slots = pl.pallas_call(
        pack_kernel,
        out_shape=jax.ShapeDtypeStruct((cols, SIZE, SIZE), BF16),
        in_specs=scalars(1) + whole(1),
        out_specs=pl.BlockSpec(memory_space=pltpu.VMEM),
        compiler_params=limit,
    )(homes, measured)
    arrived = lax.all_to_all(slots, "col", split_axis=0, concat_axis=0, tiled=True)

    taps = jnp.concatenate([tap_row, tap_col], axis=0)
    taps = jnp.concatenate([taps, taps[:, ::-1]], axis=0)
    taps = jnp.pad(taps, ((0, 0), (0, 2 * SIZE - taps.shape[1])))
    tables, adjoints = pl.pallas_call(
        table_kernel,
        out_shape=[jax.ShapeDtypeStruct((2, 2 * SIZE, 2 * SIZE), BF16) for _ in range(2)],
        in_specs=whole(1),
        out_specs=whole(2),
        compiler_params=limit,
    )(taps)
    dft_left, dft_right = dft_tables()

    def anywhere(count):
        return [pl.BlockSpec(memory_space=pl.ANY) for _ in range(count)]

    field_shape = (MODES * SIZE, 2 * SIZE)
    patch_shape = (2, SIZE, 2 * SIZE)
    work = [
        pltpu.VMEM((MODES, 2 * SIZE, SIZE), BF16),
        pltpu.VMEM(field_shape, BF16),
        pltpu.VMEM((2,) + field_shape, F32),
        pltpu.VMEM((2,) + field_shape, F32),
        pltpu.VMEM((2, SIZE, SIZE), F32),
        pltpu.VMEM((2,) + patch_shape, BF16),
    ]
    order = pltpu.SMEM((cols,), jnp.int32)
    moved_all, far_all, root_all, patch_all = pl.pallas_call(
        forward_kernel,
        out_shape=[
            jax.ShapeDtypeStruct((cols,) + field_shape, F32),
            jax.ShapeDtypeStruct((cols,) + field_shape, F32),
            jax.ShapeDtypeStruct((cols, SIZE, SIZE), F32),
            jax.ShapeDtypeStruct((cols,) + patch_shape, BF16),
        ],
        in_specs=scalars(2) + whole(7),
        out_specs=anywhere(4),
        scratch_shapes=[pltpu.VMEM((5,) + part_shape, BF16)]
        + work
        + [order, pltpu.SemaphoreType.DMA((2, 4))],
        cost_estimate=pl.CostEstimate(flops=40 * 10**9, bytes_accessed=10**7, transcendentals=0),
        compiler_params=limit,
    )(odd, codes, full, tile_low, half, probe, tables, dft_left, dft_right)
    own_grad, full_grad, half_grad, probe_part = pl.pallas_call(
        backward_kernel,
        out_shape=[
            jax.ShapeDtypeStruct(tile_shape, F32),
            jax.ShapeDtypeStruct(tile_shape, BF16),
            jax.ShapeDtypeStruct(part_shape, BF16),
            jax.ShapeDtypeStruct(probe.shape, BF16),
        ],
        in_specs=scalars(2) + whole(2) + anywhere(7),
        out_specs=anywhere(1) + whole(3),
        scratch_shapes=work
        + [
            pltpu.VMEM((2, SIZE, SIZE), BF16),
            pltpu.VMEM(probe.shape, BF16),
            pltpu.VMEM(adjoints.shape, BF16),
            pltpu.VMEM((5,) + part_shape, F32),
            pltpu.VMEM(probe.shape, F32),
            order,
            pltpu.SemaphoreType.DMA((2, 5)),
            pltpu.SemaphoreType.DMA((2,)),
            pltpu.SemaphoreType.DMA((2,)),
        ],
        compiler_params=limit,
    )(
        odd, codes, dft_left, dft_right, probe, adjoints,
        moved_all, far_all, root_all, patch_all, arrived,
    )

    full_grad = lax.ppermute(full_grad, both, ring(1))
    half_grad = lax.ppermute(half_grad, both, ring(-1))
    share = MODES * 2 * SIZE // cols
    mine = lax.all_to_all(
        probe_part.reshape(cols, share, SIZE), "col", split_axis=0, concat_axis=0, tiled=True
    )
    mine = jnp.sum(mine.astype(F32), axis=0).astype(BF16)
    mine = jnp.broadcast_to(mine[None], (rows, share, SIZE))
    mine = lax.all_to_all(mine, "row", split_axis=0, concat_axis=0, tiled=True)
    scale = 1.0 / math.sqrt(measured.shape[0] * cols * rows)
    mine = (jnp.sum(mine.astype(F32), axis=0) * scale).astype(BF16)
    mine, full_grad, half_grad = lax.optimization_barrier((mine, full_grad, half_grad))
    mine = jnp.broadcast_to(mine[None], (cols, share, SIZE))
    probe_grad = lax.all_to_all(mine, "col", split_axis=0, concat_axis=0, tiled=True)
    probe_grad = probe_grad.astype(F32).reshape(probe.shape)
    half_grad = half_grad.astype(F32)
    nothing = jnp.zeros_like(half_grad)
    odd = odd[0] == 1
    halo = [jnp.where(odd, half_grad, nothing), jnp.where(odd, nothing, half_grad)]
    return own_grad + full_grad.astype(F32) + jnp.concatenate(halo, axis=-1), probe_grad


def solution(mesh):
    in_specs = (
        P(None, None, "row", "col"),
        P(),
        P(("row", "col"), None, None),
        P(),
        P(),
        P(("row", "col"), None),
        P(("row", "col"), None),
        P("row", "col"),
    )
    out_specs = (P(None, None, "row", "col"), P())
    return jax.shard_map(body, mesh=mesh, in_specs=in_specs, out_specs=out_specs, check_vma=False)
```

profile of v0, /device:TPU:0, one launch (start us, length us, event | category | flops | bytes accessed | tf_op | source)
XLA Modules:
  0.0 182.0 jit_solution(9088365373056168709)
XLA Ops:
  0.7 0.8 copy.25
  1.4 0.1 reshape.39
  1.5 0.8 copy.26
  2.3 0.1 reshape.40
  3.0 0.6 pad_add_fusion.info
  3.6 1.5 shard_map.113
  5.1 1.4 all_to_all.20
  6.4 7.1 %all-to-all-start = ((s32[16,1,8]{2,1,0:T(1,128)}), s32[16,1,8]{2,1,0:T(1,128)S(1)}, u32[]{:S(2)}, u32[]{:S(2)}) async-start(s32[16,1,8]{2,1,0:T(1,128)} %bitcast.3), calls=%async_computation | async-start | bytes 16384 | tf_op jit(solution)/shard_map/all_to_all | solution.py:405
  13.6 2.9 %shard_map.114 = (bf16[2,2,512,256]{3,2,1,0:T(8,128)(2,1)}, bf16[2,2,512,128]{3,2,1,0:T(8,128)(2,1)}) custom-call(s32[1]{0:T(128)} %bitcast.odd, f32[2,2,512,256]{3,2,1,0:T(8,128)} %obj), custom_call_target="tpu_custom_call" | custom-call | tf_op jit(solution)/shard_map/pallas_call | solution.py:408
  16.5 4.6 %all-to-all-done = s32[16,1,8]{2,1,0:T(1,128)S(1)} async-done(((s32[16,1,8]{2,1,0:T(1,128)}), s32[16,1,8]{2,1,0:T(1,128)S(1)}, u32[]{:S(2)}, u32[]{:S(2)}) %all-to-all-start) | async-done | bytes 544 | tf_op jit(solution)/shard_map/all_to_all | solution.py:405
  21.1 0.1 copy.28
  21.1 1.8 collective-permute-start
  22.9 0.3 collective-permute-start.1
  23.2 0.1 rev.3
  23.3 0.6 select_maximum_fusion.taps
  23.9 2.5 %shard_map.116 = (bf16[2,512,512]{2,1,0:T(8,128)(2,1)}, bf16[2,512,512]{2,1,0:T(8,128)(2,1)}) custom-call(f32[8,512]{1,0:T(8,128)} %select_maximum_fusion.taps), custom_call_target="tpu_custom_call" | custom-call | tf_op jit(solution)/shard_map/pallas_call | solution.py:456
  26.4 0.1 copy.29
  26.5 0.6 reshape.42.notes
  27.1 5.2 %shard_map.115 = (s32[16]{0:T(128)}, s32[6]{0:T(128)}) custom-call(s32[1]{0:T(128)} %bitcast.1.me, s32[128]{0:T(128)} %reshape.42.notes), custom_call_target="tpu_custom_call" | custom-call | tf_op jit(solution)/shard_map/pallas_call | solution.py:430
  32.3 2.8 %shard_map.118 = bf16[16,256,256]{2,1,0:T(8,128)(2,1)} custom-call(s32[6]{0:T(128)} %get-tuple-element.38.homes, f32[6,256,256]{2,1,0:T(8,128)} %measured.1), custom_call_target="tpu_custom_call" | custom-call | tf_op jit(solution)/shard_map/pallas_call | solution.py:444
  35.1 6.5 %all-to-all-start.1 = ((bf16[16,256,256]{2,1,0:T(8,128)(2,1)}), bf16[16,256,256]{2,1,0:T(8,128)(2,1)S(1)}, u32[]{:S(2)}, u32[]{:S(2)}) async-start(bf16[16,256,256]{2,1,0:T(8,128)(2,1)} %shard_map.118), calls=%async_computation.1 | async-start | bytes 4194304 | tf_op jit(solution)/shard_map/all_to_all | solution.py:451
  41.5 0.0 collective-permute-done.1.half
  41.6 0.0 collective-permute-done.full
  41.6 1.0 copy-done.8
  42.6 13.0 %shard_map.117 = (f32[16,1024,512]{2,1,0:T(8,128)}, f32[16,1024,512]{2,1,0:T(8,128)}, f32[16,256,256]{2,1,0:T(8,128)}, bf16[16,2,256,512]{3,2,1,0:T(8,128)(2,1)}) custom-call(s32[1]{0:T(128)} %bitcast.odd, s32[16]{0:T(128)} %get-tuple-element.29.codes, bf16[2,2,512,256]{3,2,1,0:T(8,128)(2,1)} %copy-done.8, bf16[2,2,512,256]{3,2,1,0:T(8,128)(2,1)} %get-tuple-element.31.tile, ...), custom_call_target="tpu_custom_call" | custom-call | flops 40000000000 | bytes 10000000 | tf_op jit(solution)/shard_map/pallas_call | solution.py:479
  55.6 14.6 %all-to-all-done.1.slots_all = bf16[16,256,256]{2,1,0:T(8,128)(2,1)S(1)} async-done(((bf16[16,256,256]{2,1,0:T(8,128)(2,1)}), bf16[16,256,256]{2,1,0:T(8,128)(2,1)S(1)}, u32[]{:S(2)}, u32[]{:S(2)}) %all-to-all-start.1) | async-done | bytes 2097184 | tf_op jit(solution)/shard_map/all_to_all | solution.py:451
  70.2 1.3 copy-done
  71.5 15.9 %shard_map.119 = (f32[2,2,512,256]{3,2,1,0:T(8,128)}, bf16[2,2,512,256]{3,2,1,0:T(8,128)(2,1)}, bf16[2,2,512,128]{3,2,1,0:T(8,128)(2,1)}, bf16[4,2,256,256]{3,2,1,0:T(8,128)(2,1)}) custom-call(s32[1]{0:T(128)} %bitcast.odd, s32[16]{0:T(128)} %get-tuple-element.29.codes, bf16[512,512]{1,0:T(8,128)(2,1)} %constant.44.dft_left, ...), custom_call_target="tpu_custom_call" | custom-call | tf_op jit(solution)/shard_map/pallas_call | solution.py:495
  87.4 11.5 %all-to-all-start.2 = ((bf16[16,128,256]{2,1,0:T(8,128)(2,1)}), bf16[16,128,256]{2,1,0:T(8,128)(2,1)S(1)}, u32[]{:S(2)}, u32[]{:S(2)}) async-start(bf16[16,128,256]{2,1,0:T(8,128)(2,1)} %bitcast.10), calls=%async_computation.2 | async-start | bytes 2097152 | tf_op jit(solution)/shard_map/all_to_all | solution.py:526
  98.9 2.0 %collective-permute-start.2 = (bf16[2,2,512,256]{3,2,1,0:T(8,128)(2,1)S(1)}, bf16[2,2,512,256]{3,2,1,0:T(8,128)(2,1)S(1)}, u32[]{:S(2)}, u32[]{:S(2)}) collective-permute-start(bf16[2,2,512,256]{3,2,1,0:T(8,128)(2,1)S(1)} %copy-done.7), channel_id=1, source_target_pairs={{0,1},{1,2},{2,3},{3,4},{4,5},{5,6},{6,7},{7,8},{8,9},{9,10},{10,1... | collective-permute-start | bytes 3145736 | tf_op jit(solution)/shard_map/ppermute | solution.py:523
  100.9 11.2 %all-to-all-done.2 = bf16[16,128,256]{2,1,0:T(8,128)(2,1)S(1)} async-done(((bf16[16,128,256]{2,1,0:T(8,128)(2,1)}), bf16[16,128,256]{2,1,0:T(8,128)(2,1)S(1)}, u32[]{:S(2)}, u32[]{:S(2)}) %all-to-all-start.2) | async-done | bytes 1048608 | tf_op jit(solution)/shard_map/all_to_all | solution.py:526
  112.2 0.1 reduce_sum.21
  112.3 0.8 broadcast_in_dim.6
  113.1 28.8 %all-to-all-start.3 = ((bf16[8,128,256]{2,1,0:T(8,128)(2,1)}), bf16[8,128,256]{2,1,0:T(8,128)(2,1)S(1)}, u32[]{:S(2)}, u32[]{:S(2)}) async-start(bf16[8,128,256]{2,1,0:T(8,128)(2,1)} %broadcast_in_dim.6), calls=%async_computation.3 | async-start | bytes 1048576 | tf_op jit(solution)/shard_map/all_to_all | solution.py:531
  141.9 2.3 %collective-permute-start.3 = (bf16[2,2,512,128]{3,2,1,0:T(8,128)(2,1)}, bf16[2,2,512,128]{3,2,1,0:T(8,128)(2,1)S(1)}, u32[]{:S(2)}, u32[]{:S(2)}) collective-permute-start(bf16[2,2,512,128]{3,2,1,0:T(8,128)(2,1)} %get-tuple-element.42), channel_id=1, source_target_pairs={{0,15},{1,0},{2,1},{3,2},{4,3},{5,4},{6,5},{7,6},{8,7},{9,8},{10,9... | collective-permute-start | bytes 1572872 | tf_op jit(solution)/shard_map/ppermute | solution.py:524
  144.3 8.0 %all-to-all-done.3 = bf16[8,128,256]{2,1,0:T(8,128)(2,1)S(1)} async-done(((bf16[8,128,256]{2,1,0:T(8,128)(2,1)}), bf16[8,128,256]{2,1,0:T(8,128)(2,1)S(1)}, u32[]{:S(2)}, u32[]{:S(2)}) %all-to-all-start.3) | async-done | bytes 524320 | tf_op jit(solution)/shard_map/all_to_all | solution.py:531
  152.3 0.1 convert_reduce_fusion
  152.4 0.7 collective-permute-done.3
  153.1 0.8 copy-done.4
  153.9 1.0 copy-done.2
  154.9 1.1 broadcast_in_dim.8
  156.0 6.8 %all-to-all-start.4 = ((bf16[16,128,256]{2,1,0:T(8,128)(2,1)}), bf16[16,128,256]{2,1,0:T(8,128)(2,1)S(1)}, u32[]{:S(2)}, u32[]{:S(2)}) async-start(bf16[16,128,256]{2,1,0:T(8,128)(2,1)} %broadcast_in_dim.8), calls=%async_computation.4 | async-start | bytes 2097152 | tf_op jit(solution)/shard_map/all_to_all | solution.py:536
  162.8 0.0 copy-start.3
  162.8 1.3 convert_select_fusion.1
  164.1 0.1 copy-done.3
  164.2 1.7 maximum_add_fusion
  165.9 14.6 %all-to-all-done.4 = bf16[16,128,256]{2,1,0:T(8,128)(2,1)S(1)} async-done(((bf16[16,128,256]{2,1,0:T(8,128)(2,1)}), bf16[16,128,256]{2,1,0:T(8,128)(2,1)S(1)}, u32[]{:S(2)}, u32[]{:S(2)}) %all-to-all-start.4) | async-done | bytes 1048608 | tf_op jit(solution)/shard_map/all_to_all | solution.py:536
  180.5 1.5 convert.2
  (15 shorter events, 0.0 us)
Async XLA Ops:
  0.6 22.5 %copy-start.6 = (f32[2,64]{1,0:T(2,128)S(1)}, f32[2,64]{1,0:T(2,128)}, u32[]{:S(2)}) copy-start(f32[2,64]{1,0:T(2,128)} %param.13) | copy-start | bytes 1540
  0.6 22.5 %copy-start.5 = (f32[2,64]{1,0:T(2,128)S(1)}, f32[2,64]{1,0:T(2,128)}, u32[]{:S(2)}) copy-start(f32[2,64]{1,0:T(2,128)} %param.14) | copy-start | bytes 1540
  6.4 14.6 %all-to-all-start = ((s32[16,1,8]{2,1,0:T(1,128)}), s32[16,1,8]{2,1,0:T(1,128)S(1)}, u32[]{:S(2)}, u32[]{:S(2)}) async-start(s32[16,1,8]{2,1,0:T(1,128)} %bitcast.3), calls=%async_computation | async-start | bytes 16384 | tf_op jit(solution)/shard_map/all_to_all | solution.py:405
  21.1 20.5 %collective-permute-start = (bf16[2,2,512,256]{3,2,1,0:T(8,128)(2,1)}, bf16[2,2,512,256]{3,2,1,0:T(8,128)(2,1)S(1)}, u32[]{:S(2)}, u32[]{:S(2)}) collective-permute-start(bf16[2,2,512,256]{3,2,1,0:T(8,128)(2,1)} %get-tuple-element.31.tile), channel_id=1, source_target_pairs={{0,15},{1,0},{2,1},{3,2},{4,3},{5,4},{6,5},{7,6},{8,7},{9,8},{10,9... | collective-permute-start | bytes 3145736 | tf_op jit(solution)/shard_map/ppermute | solution.py:428
  22.9 18.6 %collective-permute-start.1 = (bf16[2,2,512,128]{3,2,1,0:T(8,128)(2,1)}, bf16[2,2,512,128]{3,2,1,0:T(8,128)(2,1)}, u32[]{:S(2)}, u32[]{:S(2)}) collective-permute-start(bf16[2,2,512,128]{3,2,1,0:T(8,128)(2,1)} %get-tuple-element.32), channel_id=1, source_target_pairs={{0,1},{1,2},{2,3},{3,4},{4,5},{5,6},{6,7},{7,8},{8,9},{9,10},{10,1... | collective-permute-start | bytes 1572872 | tf_op jit(solution)/shard_map/ppermute | solution.py:429
  35.1 35.1 %all-to-all-start.1 = ((bf16[16,256,256]{2,1,0:T(8,128)(2,1)}), bf16[16,256,256]{2,1,0:T(8,128)(2,1)S(1)}, u32[]{:S(2)}, u32[]{:S(2)}) async-start(bf16[16,256,256]{2,1,0:T(8,128)(2,1)} %shard_map.118), calls=%async_computation.1 | async-start | bytes 4194304 | tf_op jit(solution)/shard_map/all_to_all | solution.py:451
  41.6 1.0 copy-start.8
  70.2 1.3 copy-start
  87.4 11.5 %copy-start.7 = (bf16[2,2,512,256]{3,2,1,0:T(8,128)(2,1)S(1)}, bf16[2,2,512,256]{3,2,1,0:T(8,128)(2,1)}, u32[]{:S(2)}) copy-start(bf16[2,2,512,256]{3,2,1,0:T(8,128)(2,1)} %get-tuple-element.41) | copy-start | bytes 3145732
  87.4 24.7 %all-to-all-start.2 = ((bf16[16,128,256]{2,1,0:T(8,128)(2,1)}), bf16[16,128,256]{2,1,0:T(8,128)(2,1)S(1)}, u32[]{:S(2)}, u32[]{:S(2)}) async-start(bf16[16,128,256]{2,1,0:T(8,128)(2,1)} %bitcast.10), calls=%async_computation.2 | async-start | bytes 2097152 | tf_op jit(solution)/shard_map/all_to_all | solution.py:526
  98.9 54.2 %collective-permute-start.2 = (bf16[2,2,512,256]{3,2,1,0:T(8,128)(2,1)S(1)}, bf16[2,2,512,256]{3,2,1,0:T(8,128)(2,1)S(1)}, u32[]{:S(2)}, u32[]{:S(2)}) collective-permute-start(bf16[2,2,512,256]{3,2,1,0:T(8,128)(2,1)S(1)} %copy-done.7), channel_id=1, source_target_pairs={{0,1},{1,2},{2,3},{3,4},{4,5},{5,6},{6,7},{7,8},{8,9},{9,10},{10,1... | collective-permute-start | bytes 3145736 | tf_op jit(solution)/shard_map/ppermute | solution.py:523
  113.1 39.2 %all-to-all-start.3 = ((bf16[8,128,256]{2,1,0:T(8,128)(2,1)}), bf16[8,128,256]{2,1,0:T(8,128)(2,1)S(1)}, u32[]{:S(2)}, u32[]{:S(2)}) async-start(bf16[8,128,256]{2,1,0:T(8,128)(2,1)} %broadcast_in_dim.6), calls=%async_computation.3 | async-start | bytes 1048576 | tf_op jit(solution)/shard_map/all_to_all | solution.py:531
  141.9 11.2 %collective-permute-start.3 = (bf16[2,2,512,128]{3,2,1,0:T(8,128)(2,1)}, bf16[2,2,512,128]{3,2,1,0:T(8,128)(2,1)S(1)}, u32[]{:S(2)}, u32[]{:S(2)}) collective-permute-start(bf16[2,2,512,128]{3,2,1,0:T(8,128)(2,1)} %get-tuple-element.42), channel_id=1, source_target_pairs={{0,15},{1,0},{2,1},{3,2},{4,3},{5,4},{6,5},{7,6},{8,7},{9,8},{10,9... | collective-permute-start | bytes 1572872 | tf_op jit(solution)/shard_map/ppermute | solution.py:524
  153.1 0.8 copy-start.4
  153.9 1.0 copy-start.2
  156.0 8.1 %copy-start.1 = (f32[2,2,512,256]{3,2,1,0:T(8,128)S(1)}, f32[2,2,512,256]{3,2,1,0:T(8,128)}, u32[]{:S(2)}) copy-start(f32[2,2,512,256]{3,2,1,0:T(8,128)} %get-tuple-element.39) | copy-start | bytes 6291460
  156.0 24.5 %all-to-all-start.4 = ((bf16[16,128,256]{2,1,0:T(8,128)(2,1)}), bf16[16,128,256]{2,1,0:T(8,128)(2,1)S(1)}, u32[]{:S(2)}, u32[]{:S(2)}) async-start(bf16[16,128,256]{2,1,0:T(8,128)(2,1)} %broadcast_in_dim.8), calls=%async_computation.4 | async-start | bytes 2097152 | tf_op jit(solution)/shard_map/all_to_all | solution.py:536
  162.8 1.4 copy-start.3
where the time goes:
time: 181 us; the launch traced here: 182 us
  starting transfers between devices  67 us (37%)
  waiting for transfers between devices  53.8 us (30%)
  Pallas kernels  43.8 us (24%)
  local copies, waits for them, and re-layouts  9.98 us (6%)
  other arithmetic  5.95 us (3%)
    all_to_all x1, starting transfers between devices, body(): mine = lax.all_to_all(mine, 'row', split_axis=0, concat_axis=0, tiled=True)  28.8 us
    pallas_call x1, Pallas kernels, body(): pl.pallas_call(backward_kernel, out_shape=[jax.ShapeDtypeStruct(tile_shap...  15.9 us
    all_to_all x1, waiting for transfers between devices, body(): lax.all_to_all(mine, 'col', split_axis=0, concat_axis=0, tiled=True)  14.6 us
    all_to_all x1, waiting for transfers between devices, body(): lax.all_to_all(slots, 'col', split_axis=0, concat_axis=0, tiled=True)  14.6 us
    pallas_call x1, Pallas kernels, body(): pl.pallas_call(forward_kernel, out_shape=[jax.ShapeDtypeStruct((cols,) +...  13 us
    all_to_all x1, starting transfers between devices, body(): lax.all_to_all(probe_part.reshape(cols, share, SIZE), 'col', split_axis=0...  11.5 us
    all_to_all x1, waiting for transfers between devices, body(): lax.all_to_all(probe_part.reshape(cols, share, SIZE), 'col', split_axis=0...  11.2 us
    all_to_all x1, waiting for transfers between devices, body(): mine = lax.all_to_all(mine, 'row', split_axis=0, concat_axis=0, tiled=True)  8 us
  transfers between devices with their start and end apart: 9, of which 6 were waited for; matrix products, arithmetic and copies ran while one was open for 3% of the time, Pallas kernels for 15%

commit v1 on v0

--- a/solution.py
+++ b/solution.py
@@ -41,13 +41,11 @@
             same = (tile[one] == tile[two]) & (straddles[one] + straddles[two] == 2)
             same = same.astype(jnp.int32)
             before[two], after[one] = before[two] | same, after[one] | same
-    owner = [tile[n] + before[n] for n in range(scans)]
     odd = info[4 * scans + 1]
-    aside = 2 * odd - 1
-    other = [
-        lax.rem(tile[n] + straddles[n] + (1 - straddles[n]) * aside + tiles, tiles)
-        for n in range(scans)
-    ]
+    shift = [straddles[n] * jnp.where(odd == 1, 1 - after[n], before[n]) for n in range(scans)]
+    owner = [tile[n] + shift[n] for n in range(scans)]
+    aside = [jnp.where(straddles[n] == 1, 1 - shift[n], 2 * odd - 1) for n in range(scans)]
+    other = [lax.rem(tile[n] + aside[n] + tiles, tiles) for n in range(scans)]
     for n in range(scans):
         free = live[n] * (1 - before[n]) * (1 - after[n])
         for k in range(scans):
@@ -55,8 +53,8 @@
                 free = free * (1 - (owner[k] == other[n]).astype(jnp.int32))
             if k < n:
                 free = free * (1 - (other[k] == other[n]).astype(jnp.int32))
-        column = (1 + straddles[n] - 2 * before[n] + odd) & 3
-        moved_column = (3 * (1 - straddles[n]) + odd) & 3
+        column = (jnp.where(straddles[n] == 1, 2 - 2 * shift[n], 1) + odd) & 3
+        moved_column = (jnp.where(straddles[n] == 1, 2 * shift[n], 3) + odd) & 3
         note = live[n] + 2 * free + 4 * owner[n] + 64 * other[n] + 1024 * level[n]
         note = note + 4096 * column + 16384 * moved_column
         for t in range(tiles):
@@ -66,52 +64,36 @@
             notes[t * SLOTS + n] = 0
 
 
-def assign_kernel(me, notes, codes, homes, loads, moves):
+def assign_kernel(me, notes, codes, homes, loads):
     tiles = codes.shape[0]
     scans = homes.shape[0]
     for t in range(tiles):
         loads[t] = 0
-        codes[t] = 0
-
-    def fields(place):
-        note = notes[place]
-        return note & 1, (note >> 1) & 1, (note >> 2) & 15, (note >> 6) & 15, note
 
     @pl.loop(0, tiles)
     def _(source):
         for n in range(scans):
-            live, _, owner, _, _ = fields(source * SLOTS + n)
-            loads[owner] += live
-            moves[source * SLOTS + n] = 0
-
-    for _ in range(2):
-
-        @pl.loop(0, tiles)
-        def _(source):
-            for n in range(scans):
-                place = source * SLOTS + n
-                _, free, owner, other, _ = fields(place)
-                gain = (loads[owner] > loads[other] + 1).astype(jnp.int32)
-                step = free * gain * (1 - moves[place])
-                loads[owner] -= step
-                loads[other] += step
-                moves[place] += step
+            note = notes[source * SLOTS + n]
+            loads[(note >> 2) & 15] += note & 1
 
     @pl.loop(0, tiles)
     def _(source):
         code = jnp.int32(0)
         for n in range(scans):
-            place = source * SLOTS + n
-            live, _, owner, other, note = fields(place)
-            moved = moves[place] == 1
-            home = jnp.where(moved, other, owner)
-            column = jnp.where(moved, (note >> 14) & 3, (note >> 12) & 3)
-            here = live * (home == me[0]).astype(jnp.int32)
-            code = code + here * (1 + 4 * ((note >> 10) & 3) + column)
+            note = notes[source * SLOTS + n]
+            owner, other = (note >> 2) & 15, (note >> 6) & 15
+            here, there = loads[owner], loads[other]
+            move = ((note >> 1) & 1) * (here > there + 1).astype(jnp.int32)
+            loads[owner] = here - move
+            loads[other] = loads[other] + move
+            home = jnp.where(move == 1, other, owner)
+            column = (note >> (12 + 2 * move)) & 3
+            mine = (note & 1) * (home == me[0]).astype(jnp.int32)
+            code = code + mine * (1 + 4 * ((note >> 10) & 3) + column)
 
             @pl.when(source == me[0])
             def _():
-                homes[n] = jnp.where(live == 1, home, -1)
+                homes[n] = jnp.where((note & 1) == 1, home, -1)
 
         codes[source] = code
 
@@ -130,46 +112,51 @@
             slots[homes[n]] = measured[n].astype(BF16)
 
 
-def table_kernel(taps, tables, adjoints):
-    def banded(row, shift):
-        line = jnp.broadcast_to(taps[row : row + 1, :], (SIZE, 2 * SIZE))
-        return pltpu.roll(line, shift, 1, stride=1, stride_axis=0)[:, :SIZE]
-
-    straight, turned = 2 * SIZE - 32, 2 * SIZE - 31
-
-    def put(out, real, imag, from_left):
-        sign = 1.0 if from_left else -1.0
-        out[:SIZE, :SIZE] = real.astype(BF16)
-        out[:SIZE, SIZE:] = (-sign * imag).astype(BF16)
-        out[SIZE:, :SIZE] = (sign * imag).astype(BF16)
-        out[SIZE:, SIZE:] = real.astype(BF16)
-
-    put(tables.at[0], banded(0, straight), banded(1, straight), True)
-    put(tables.at[1], banded(6, turned), banded(7, turned), False)
-    put(adjoints.at[0], banded(4, turned), -banded(5, turned), True)
-    put(adjoints.at[1], banded(2, straight), -banded(3, straight), False)
+def banded(taps, row, shift):
+    line = jnp.broadcast_to(taps[row : row + 1, :], (SIZE, 2 * SIZE))
+    return pltpu.roll(line, shift, 1, stride=1, stride_axis=0)[:, :SIZE]
+
+
+STRAIGHT, TURNED = 2 * SIZE - 32, 2 * SIZE - 31
+
+
+def put_table(out, real, imag, from_left):
+    sign = 1.0 if from_left else -1.0
+    out[:SIZE, :SIZE] = real.astype(BF16)
+    out[:SIZE, SIZE:] = (-sign * imag).astype(BF16)
+    out[SIZE:, :SIZE] = (sign * imag).astype(BF16)
+    out[SIZE:, SIZE:] = real.astype(BF16)
+
+
+def put_tables(taps, tables):
+    put_table(tables.at[0], banded(taps, 0, STRAIGHT), banded(taps, 1, STRAIGHT), True)
+    put_table(tables.at[1], banded(taps, 6, TURNED), banded(taps, 7, TURNED), False)
+
+
+def put_adjoints(taps, tables):
+    put_table(tables.at[0], banded(taps, 4, TURNED), -banded(taps, 5, TURNED), True)
+    put_table(tables.at[1], banded(taps, 2, STRAIGHT), -banded(taps, 3, STRAIGHT), False)
 
 
 CHUNKS = [slice(at, at + CHUNK) for at in range(0, SIZE, CHUNK)]
 
 
 def left_stage(table, rows_in, cols_in):
+    both = jnp.dot(table, rows_in[...], preferred_element_type=F32).astype(BF16)
     for m in range(MODES):
-        both = jnp.dot(table, rows_in[m], preferred_element_type=F32)
-        here = slice(m * SIZE, (m + 1) * SIZE)
-        cols_in[here, :SIZE] = both[:SIZE].astype(BF16)
-        cols_in[here, SIZE:] = both[SIZE:].astype(BF16)
+        rows, cols = slice(m * SIZE, (m + 1) * SIZE), slice(m * SIZE, (m + 1) * SIZE)
+        cols_in[rows, :SIZE] = both[:SIZE, cols]
+        cols_in[rows, SIZE:] = both[SIZE:, cols]
 
 
 def right_stage(table, cols_in, out):
-    for m in range(MODES):
-        here = slice(m * SIZE, (m + 1) * SIZE)
-        out[here, :] = jnp.dot(cols_in[here, :], table, preferred_element_type=F32)
+    out[...] = jnp.dot(cols_in[...], table, preferred_element_type=F32)
 
 
 def put_rows(rows_in, m, at, real, imag):
-    rows_in[m, at.start : at.stop, :] = real.astype(BF16)
-    rows_in[m, SIZE + at.start : SIZE + at.stop, :] = imag.astype(BF16)
+    cols = slice(m * SIZE, (m + 1) * SIZE)
+    rows_in[at.start : at.stop, cols] = real.astype(BF16)
+    rows_in[SIZE + at.start : SIZE + at.stop, cols] = imag.astype(BF16)
 
 
 def pair(ref, m, at):
@@ -205,11 +192,12 @@
 
 
 def forward_kernel(
-    odd, codes, full, tile, half, probe, tables, dft_left, dft_right,
+    odd, codes, full, tile, half, probe, taps, dft_left, dft_right,
     moved_all, far_all, root_all, patch_all,
-    ext, rows_in, cols_in, moved_two, far_two, root_two, patch_two, order, sems,
+    ext, tables, rows_in, cols_in, moved_two, far_two, root_two, patch_two, order, sems,
 ):
     extend(odd[0], full, tile, half, ext)
+    put_tables(taps, tables)
     found = live_list(codes, order)
     wholes = (moved_all, far_all, root_all, patch_all)
     buffers = (moved_two, far_two, root_two, patch_two)
@@ -269,7 +257,7 @@
 
 
 def backward_kernel(
-    odd, codes, dft_left, dft_right, probe_all, adjoints_all,
+    odd, codes, dft_left, dft_right, taps, probe_all,
     moved_all, far_all, root_all, patch_all, slots_all,
     own_grad, full_grad, half_grad, probe_grad,
     rows_in, cols_in, moved_two, far_two, root_two, patch_two, slots_two,
@@ -278,10 +266,7 @@
     found = live_list(codes, order)
     wholes = (far_all, slots_all, root_all, moved_all, patch_all)
     buffers = (far_two, slots_two, root_two, moved_two, patch_two)
-    tables = [
-        pltpu.make_async_copy(probe_all, probe, once.at[0]),
-        pltpu.make_async_copy(adjoints_all, adjoints, once.at[1]),
-    ]
+    probe_copy = pltpu.make_async_copy(probe_all, probe, once)
 
     def copies(i):
         two = lax.rem(i, 2)
@@ -292,9 +277,10 @@
 
     @pl.when(found > 0)
     def _():
-        for copy in copies(0) + tables:
+        for copy in copies(0) + [probe_copy]:
             copy.start()
 
+    put_adjoints(taps, adjoints)
     acc[...] = jnp.zeros(acc.shape, F32)
     probe_acc[...] = jnp.zeros(probe_acc.shape, F32)
 
@@ -337,13 +323,13 @@
                 put_rows(rows_in, m, at, o_re * a_re + o_im * a_im, o_re * a_im - o_im * a_re)
             add_piece(1, at, column, start, g_re, g_im)
 
+        left_stage(adjoints[0], rows_in, cols_in)
+        right_stage(adjoints[1], cols_in, moved)
+
         @pl.when(i == 0)
         def _():
-            for copy in tables:
-                copy.wait()
-
-        left_stage(adjoints[0], rows_in, cols_in)
-        right_stage(adjoints[1], cols_in, moved)
+            probe_copy.wait()
+
         for at in CHUNKS:
             o_re, o_im = pair_of(patch, 0, at)
             g_re = jnp.zeros((CHUNK, SIZE), F32)
@@ -435,10 +421,7 @@
         ],
         in_specs=scalars(2),
         out_specs=scalars(2),
-        scratch_shapes=[
-            pltpu.SMEM((cols,), jnp.int32),
-            pltpu.SMEM((cols * SLOTS,), jnp.int32),
-        ],
+        scratch_shapes=[pltpu.SMEM((cols,), jnp.int32)],
         compiler_params=limit,
     )(lax.axis_index("col").reshape(1), row_notes.reshape(cols * SLOTS))
     slots = pl.pallas_call(
@@ -453,13 +436,6 @@
     taps = jnp.concatenate([tap_row, tap_col], axis=0)
     taps = jnp.concatenate([taps, taps[:, ::-1]], axis=0)
     taps = jnp.pad(taps, ((0, 0), (0, 2 * SIZE - taps.shape[1])))
-    tables, adjoints = pl.pallas_call(
-        table_kernel,
-        out_shape=[jax.ShapeDtypeStruct((2, 2 * SIZE, 2 * SIZE), BF16) for _ in range(2)],
-        in_specs=whole(1),
-        out_specs=whole(2),
-        compiler_params=limit,
-    )(taps)
     dft_left, dft_right = dft_tables()
 
     def anywhere(count):
@@ -467,8 +443,9 @@
 
     field_shape = (MODES * SIZE, 2 * SIZE)
     patch_shape = (2, SIZE, 2 * SIZE)
+    pair_shape = (2, 2 * SIZE, 2 * SIZE)
     work = [
-        pltpu.VMEM((MODES, 2 * SIZE, SIZE), BF16),
+        pltpu.VMEM((2 * SIZE, MODES * SIZE), BF16),
         pltpu.VMEM(field_shape, BF16),
         pltpu.VMEM((2,) + field_shape, F32),
         pltpu.VMEM((2,) + field_shape, F32),
@@ -486,12 +463,12 @@
         ],
         in_specs=scalars(2) + whole(7),
         out_specs=anywhere(4),
-        scratch_shapes=[pltpu.VMEM((5,) + part_shape, BF16)]
+        scratch_shapes=[pltpu.VMEM((5,) + part_shape, BF16), pltpu.VMEM(pair_shape, BF16)]
         + work
         + [order, pltpu.SemaphoreType.DMA((2, 4))],
         cost_estimate=pl.CostEstimate(flops=40 * 10**9, bytes_accessed=10**7, transcendentals=0),
         compiler_params=limit,
-    )(odd, codes, full, tile_low, half, probe, tables, dft_left, dft_right)
+    )(odd, codes, full, tile_low, half, probe, taps, dft_left, dft_right)
     own_grad, full_grad, half_grad, probe_part = pl.pallas_call(
         backward_kernel,
         out_shape=[
@@ -500,23 +477,23 @@
             jax.ShapeDtypeStruct(part_shape, BF16),
             jax.ShapeDtypeStruct(probe.shape, BF16),
         ],
-        in_specs=scalars(2) + whole(2) + anywhere(7),
+        in_specs=scalars(2) + whole(3) + anywhere(6),
         out_specs=anywhere(1) + whole(3),
         scratch_shapes=work
         + [
             pltpu.VMEM((2, SIZE, SIZE), BF16),
             pltpu.VMEM(probe.shape, BF16),
-            pltpu.VMEM(adjoints.shape, BF16),
+            pltpu.VMEM(pair_shape, BF16),
             pltpu.VMEM((5,) + part_shape, F32),
             pltpu.VMEM(probe.shape, F32),
             order,
             pltpu.SemaphoreType.DMA((2, 5)),
-            pltpu.SemaphoreType.DMA((2,)),
+            pltpu.SemaphoreType.DMA,
             pltpu.SemaphoreType.DMA((2,)),
         ],
         compiler_params=limit,
     )(
-        odd, codes, dft_left, dft_right, probe, adjoints,
+        odd, codes, dft_left, dft_right, taps, probe,
         moved_all, far_all, root_all, patch_all, arrived,
     )
 

time: 181 us -> 173 us (0.956); the launches traced: 182 us -> 172 us
  starting transfers between devices: 67 us -> 52.5 us
  Pallas kernels: 43.8 us -> 46.1 us
    all_to_all x1, starting transfers between devices: 28.8 us -> 12.9 us  [body(): mine = lax.all_to_all(mine, 'row', split_axis=0, concat_axis=0, tiled=True)]
    all_to_all x1, waiting for transfers between devices: 14.6 us -> 0.01 us  [body(): lax.all_to_all(slots, 'col', split_axis=0, concat_axis=0, tiled=True)]
    ppermute x1, waiting for transfers between devices: 0.05 us -> 12 us  [body(): full = lax.ppermute(tile_low, both, ring(-1))]
    ppermute x1, starting transfers between devices: 2.35 us -> 11.1 us  [body(): half_grad = lax.ppermute(half_grad, both, ring(-1))]
    all_to_all x1, waiting for transfers between devices: 8 us -> 0.01 us  [body(): mine = lax.all_to_all(mine, 'row', split_axis=0, concat_axis=0, tiled=True)]
    all_to_all x1, starting transfers between devices: 11.5 us -> 3.8 us  [body(): lax.all_to_all(probe_part.reshape(cols, share, SIZE), 'col', split_axis=0...]
    ppermute x1, waiting for transfers between devices: 0.72 us -> 6.92 us  [body(): half_grad = lax.ppermute(half_grad, both, ring(-1))]
    ppermute x1, waiting for transfers between devices: 0.01 us -> 5.76 us  [body(): half = lax.ppermute(half, both, ring(1))]
  transfers between devices with their start and end apart: 9 -> 9, of which waited for: 6 -> 6; matrix products, arithmetic and copies ran while one was open for 3% -> 3% of each run, Pallas kernels for 15% -> 14%
where the time goes in v1:
time: 173 us; the launch traced here: 172 us
  waiting for transfers between devices  55.6 us (32%)
  starting transfers between devices  52.5 us (30%)
  Pallas kernels  46.1 us (27%)
  local copies, waits for them, and re-layouts  10 us (6%)
  other arithmetic  5.94 us (3%)
    pallas_call x1, Pallas kernels, body(): pl.pallas_call(backward_kernel, out_shape=[jax.ShapeDtypeStruct(tile_shap...  20.3 us
    pallas_call x1, Pallas kernels, body(): pl.pallas_call(forward_kernel, out_shape=[jax.ShapeDtypeStruct((cols,) +...  15.5 us
    all_to_all x1, waiting for transfers between devices, body(): lax.all_to_all(probe_part.reshape(cols, share, SIZE), 'col', split_axis=0...  14.8 us
    all_to_all x1, starting transfers between devices, body(): mine = lax.all_to_all(mine, 'row', split_axis=0, concat_axis=0, tiled=True)  12.9 us
    ppermute x1, waiting for transfers between devices, body(): full = lax.ppermute(tile_low, both, ring(-1))  12 us
    all_to_all x1, waiting for transfers between devices, body(): lax.all_to_all(mine, 'col', split_axis=0, concat_axis=0, tiled=True)  11.6 us
    ppermute x1, starting transfers between devices, body(): half_grad = lax.ppermute(half_grad, both, ring(-1))  11.1 us
    all_to_all x1, starting transfers between devices, body(): lax.all_to_all(mine, 'col', split_axis=0, concat_axis=0, tiled=True)  7.21 us
  transfers between devices with their start and end apart: 9, of which 6 were waited for; matrix products, arithmetic and copies ran while one was open for 3% of the time, Pallas kernels for 14%

profile of v1, /device:TPU:0, one launch (start us, length us, event | category | flops | bytes accessed | tf_op | source)
XLA Modules:
  0.0 171.6 jit_solution(13525158334904326272)
XLA Ops:
  0.7 0.8 copy.25
  1.4 0.1 reshape.39
  1.5 0.8 copy.26
  2.3 0.1 reshape.40
  3.0 0.6 pad_add_fusion.info
  3.6 1.5 shard_map.113
  5.1 1.3 all_to_all.20
  6.4 7.1 %all-to-all-start = ((s32[16,1,8]{2,1,0:T(1,128)}), s32[16,1,8]{2,1,0:T(1,128)S(1)}, u32[]{:S(2)}, u32[]{:S(2)}) async-start(s32[16,1,8]{2,1,0:T(1,128)} %bitcast.3), calls=%async_computation | async-start | bytes 16384 | tf_op jit(solution)/shard_map/all_to_all | solution.py:391
  13.5 2.9 %shard_map.114 = (bf16[2,2,512,256]{3,2,1,0:T(8,128)(2,1)}, bf16[2,2,512,128]{3,2,1,0:T(8,128)(2,1)}) custom-call(s32[1]{0:T(128)} %bitcast.odd, f32[2,2,512,256]{3,2,1,0:T(8,128)} %obj), custom_call_target="tpu_custom_call" | custom-call | tf_op jit(solution)/shard_map/pallas_call | solution.py:394
  16.5 4.6 %all-to-all-done = s32[16,1,8]{2,1,0:T(1,128)S(1)} async-done(((s32[16,1,8]{2,1,0:T(1,128)}), s32[16,1,8]{2,1,0:T(1,128)S(1)}, u32[]{:S(2)}, u32[]{:S(2)}) %all-to-all-start) | async-done | bytes 544 | tf_op jit(solution)/shard_map/all_to_all | solution.py:391
  21.0 0.1 copy.28
  21.1 1.8 %collective-permute-start = (bf16[2,2,512,256]{3,2,1,0:T(8,128)(2,1)}, bf16[2,2,512,256]{3,2,1,0:T(8,128)(2,1)S(1)}, u32[]{:S(2)}, u32[]{:S(2)}) collective-permute-start(bf16[2,2,512,256]{3,2,1,0:T(8,128)(2,1)} %get-tuple-element.28.tile), channel_id=1, source_target_pairs={{0,15},{1,0},{2,1},{3,2},{4,3},{5,4},{6,5},{7,6},{8,7},{9,8},{10,9... | collective-permute-start | bytes 3145736 | tf_op jit(solution)/shard_map/ppermute | solution.py:414
  22.9 0.3 collective-permute-start.1
  23.1 0.1 rev.3
  23.2 0.6 select_maximum_fusion.taps
  23.9 0.1 copy.29
  23.9 0.6 reshape.42.notes
  24.5 3.0 %shard_map.115 = (s32[16]{0:T(128)}, s32[6]{0:T(128)}) custom-call(s32[1]{0:T(128)} %bitcast.1.me, s32[128]{0:T(128)} %reshape.42.notes), custom_call_target="tpu_custom_call" | custom-call | tf_op jit(solution)/shard_map/pallas_call | solution.py:416
  27.6 2.9 %shard_map.117 = bf16[16,256,256]{2,1,0:T(8,128)(2,1)} custom-call(s32[6]{0:T(128)} %get-tuple-element.34.homes, f32[6,256,256]{2,1,0:T(8,128)} %measured.1), custom_call_target="tpu_custom_call" | custom-call | tf_op jit(solution)/shard_map/pallas_call | solution.py:427
  30.4 6.5 %all-to-all-start.1 = ((bf16[16,256,256]{2,1,0:T(8,128)(2,1)}), bf16[16,256,256]{2,1,0:T(8,128)(2,1)S(1)}, u32[]{:S(2)}, u32[]{:S(2)}) async-start(bf16[16,256,256]{2,1,0:T(8,128)(2,1)} %shard_map.117), calls=%async_computation.1 | async-start | bytes 4194304 | tf_op jit(solution)/shard_map/all_to_all | solution.py:434
  36.9 5.8 %collective-permute-done.1.half = bf16[2,2,512,128]{3,2,1,0:T(8,128)(2,1)} collective-permute-done((bf16[2,2,512,128]{3,2,1,0:T(8,128)(2,1)}, bf16[2,2,512,128]{3,2,1,0:T(8,128)(2,1)}, u32[]{:S(2)}, u32[]{:S(2)}) %collective-permute-start.1) | collective-permute-done | bytes 524320 | tf_op jit(solution)/shard_map/ppermute | solution.py:415
  42.7 12.0 %collective-permute-done.full = bf16[2,2,512,256]{3,2,1,0:T(8,128)(2,1)S(1)} collective-permute-done((bf16[2,2,512,256]{3,2,1,0:T(8,128)(2,1)}, bf16[2,2,512,256]{3,2,1,0:T(8,128)(2,1)S(1)}, u32[]{:S(2)}, u32[]{:S(2)}) %collective-permute-start) | collective-permute-done | bytes 1048608 | tf_op jit(solution)/shard_map/ppermute | solution.py:414
  54.6 1.1 copy-done.8
  55.7 15.5 %shard_map.116 = (f32[16,1024,512]{2,1,0:T(8,128)}, f32[16,1024,512]{2,1,0:T(8,128)}, f32[16,256,256]{2,1,0:T(8,128)}, bf16[16,2,256,512]{3,2,1,0:T(8,128)(2,1)}) custom-call(s32[1]{0:T(128)} %bitcast.odd, s32[16]{0:T(128)} %get-tuple-element.27.codes, bf16[2,2,512,256]{3,2,1,0:T(8,128)(2,1)} %copy-done.8, bf16[2,2,512,256]{3,2,1,0:T(8,128)(2,1)} %get-tuple-element.28.tile, ...), custom_call_target="tpu_custom_call" | custom-call | flops 40000000000 | bytes 10000000 | tf_op jit(solution)/shard_map/pallas_call | solution.py:456
  71.3 0.0 copy-start
  71.3 1.3 copy-done
  72.6 20.3 %shard_map.118 = (f32[2,2,512,256]{3,2,1,0:T(8,128)}, bf16[2,2,512,256]{3,2,1,0:T(8,128)(2,1)}, bf16[2,2,512,128]{3,2,1,0:T(8,128)(2,1)}, bf16[4,2,256,256]{3,2,1,0:T(8,128)(2,1)}) custom-call(s32[1]{0:T(128)} %bitcast.odd, s32[16]{0:T(128)} %get-tuple-element.27.codes, bf16[512,512]{1,0:T(8,128)(2,1)} %constant.44.dft_left, ...), custom_call_target="tpu_custom_call" | custom-call | tf_op jit(solution)/shard_map/pallas_call | solution.py:472
  92.9 3.8 %all-to-all-start.2 = ((bf16[16,128,256]{2,1,0:T(8,128)(2,1)}), bf16[16,128,256]{2,1,0:T(8,128)(2,1)S(1)}, u32[]{:S(2)}, u32[]{:S(2)}) async-start(bf16[16,128,256]{2,1,0:T(8,128)(2,1)} %bitcast.10), calls=%async_computation.2 | async-start | bytes 2097152 | tf_op jit(solution)/shard_map/all_to_all | solution.py:503
  96.7 1.9 %collective-permute-start.2 = (bf16[2,2,512,256]{3,2,1,0:T(8,128)(2,1)S(1)}, bf16[2,2,512,256]{3,2,1,0:T(8,128)(2,1)S(1)}, u32[]{:S(2)}, u32[]{:S(2)}) collective-permute-start(bf16[2,2,512,256]{3,2,1,0:T(8,128)(2,1)S(1)} %copy-done.7), channel_id=1, source_target_pairs={{0,1},{1,2},{2,3},{3,4},{4,5},{5,6},{6,7},{7,8},{8,9},{9,10},{10,1... | collective-permute-start | bytes 3145736 | tf_op jit(solution)/shard_map/ppermute | solution.py:500
  98.6 14.8 %all-to-all-done.2 = bf16[16,128,256]{2,1,0:T(8,128)(2,1)S(1)} async-done(((bf16[16,128,256]{2,1,0:T(8,128)(2,1)}), bf16[16,128,256]{2,1,0:T(8,128)(2,1)S(1)}, u32[]{:S(2)}, u32[]{:S(2)}) %all-to-all-start.2) | async-done | bytes 1048608 | tf_op jit(solution)/shard_map/all_to_all | solution.py:503
  113.3 0.1 reduce_sum.21
  113.5 0.8 broadcast_in_dim.6
  114.3 12.9 %all-to-all-start.3 = ((bf16[8,128,256]{2,1,0:T(8,128)(2,1)}), bf16[8,128,256]{2,1,0:T(8,128)(2,1)S(1)}, u32[]{:S(2)}, u32[]{:S(2)}) async-start(bf16[8,128,256]{2,1,0:T(8,128)(2,1)} %broadcast_in_dim.6), calls=%async_computation.3 | async-start | bytes 1048576 | tf_op jit(solution)/shard_map/all_to_all | solution.py:508
  127.2 11.1 %collective-permute-start.3 = (bf16[2,2,512,128]{3,2,1,0:T(8,128)(2,1)}, bf16[2,2,512,128]{3,2,1,0:T(8,128)(2,1)S(1)}, u32[]{:S(2)}, u32[]{:S(2)}) collective-permute-start(bf16[2,2,512,128]{3,2,1,0:T(8,128)(2,1)} %get-tuple-element.38), channel_id=1, source_target_pairs={{0,15},{1,0},{2,1},{3,2},{4,3},{5,4},{6,5},{7,6},{8,7},{9,8},{10,9... | collective-permute-start | bytes 1572872 | tf_op jit(solution)/shard_map/ppermute | solution.py:501
  138.3 0.0 all-to-all-done.3
  138.3 0.1 convert_reduce_fusion
  138.4 6.9 %collective-permute-done.3 = bf16[2,2,512,128]{3,2,1,0:T(8,128)(2,1)S(1)} collective-permute-done((bf16[2,2,512,128]{3,2,1,0:T(8,128)(2,1)}, bf16[2,2,512,128]{3,2,1,0:T(8,128)(2,1)S(1)}, u32[]{:S(2)}, u32[]{:S(2)}) %collective-permute-start.3) | collective-permute-done | bytes 524320 | tf_op jit(solution)/shard_map/ppermute | solution.py:501
  145.3 0.0 collective-permute-done.2
  145.3 0.8 copy-done.4
  146.1 1.0 copy-done.2
  147.1 1.1 broadcast_in_dim.8
  148.2 7.2 %all-to-all-start.4 = ((bf16[16,128,256]{2,1,0:T(8,128)(2,1)}), bf16[16,128,256]{2,1,0:T(8,128)(2,1)S(1)}, u32[]{:S(2)}, u32[]{:S(2)}) async-start(bf16[16,128,256]{2,1,0:T(8,128)(2,1)} %broadcast_in_dim.8), calls=%async_computation.4 | async-start | bytes 2097152 | tf_op jit(solution)/shard_map/all_to_all | solution.py:513
  155.4 0.0 copy-start.3
  155.4 1.3 convert_select_fusion.1
  156.7 0.1 copy-done.3
  156.8 1.7 %maximum_add_fusion = f32[2,2,512,256]{3,2,1,0:T(8,128)} fusion(f32[2,2,512,128]{3,2,1,0:T(8,128)S(1)} %get-tuple-element.43, f32[2,2,512,128]{3,2,1,0:T(8,128)S(1)} %get-tuple-element.42, f32[2,2,512,256]{3,2,1,0:T(8,128)S(1)} %copy-done.1, bf16[2,2,512,256]{3,2,1,0:T(8,128)(2,1)S(1)} %copy-done.3), kind=kLoop, calls=%fused_computation | loop fusion | flops 2097152 | bytes 7340032 | tf_op jit(solution)/shard_map/add | solution.py:519
  158.5 11.6 %all-to-all-done.4 = bf16[16,128,256]{2,1,0:T(8,128)(2,1)S(1)} async-done(((bf16[16,128,256]{2,1,0:T(8,128)(2,1)}), bf16[16,128,256]{2,1,0:T(8,128)(2,1)S(1)}, u32[]{:S(2)}, u32[]{:S(2)}) %all-to-all-start.4) | async-done | bytes 1048608 | tf_op jit(solution)/shard_map/all_to_all | solution.py:513
  170.1 1.5 convert.2
  (14 shorter events, 0.0 us)
Async XLA Ops:
  0.6 22.5 %copy-start.6 = (f32[2,64]{1,0:T(2,128)S(1)}, f32[2,64]{1,0:T(2,128)}, u32[]{:S(2)}) copy-start(f32[2,64]{1,0:T(2,128)} %param.13) | copy-start | bytes 1540
  0.6 22.5 %copy-start.5 = (f32[2,64]{1,0:T(2,128)S(1)}, f32[2,64]{1,0:T(2,128)}, u32[]{:S(2)}) copy-start(f32[2,64]{1,0:T(2,128)} %param.14) | copy-start | bytes 1540
  6.4 14.6 %all-to-all-start = ((s32[16,1,8]{2,1,0:T(1,128)}), s32[16,1,8]{2,1,0:T(1,128)S(1)}, u32[]{:S(2)}, u32[]{:S(2)}) async-start(s32[16,1,8]{2,1,0:T(1,128)} %bitcast.3), calls=%async_computation | async-start | bytes 16384 | tf_op jit(solution)/shard_map/all_to_all | solution.py:391
  21.1 33.5 %collective-permute-start = (bf16[2,2,512,256]{3,2,1,0:T(8,128)(2,1)}, bf16[2,2,512,256]{3,2,1,0:T(8,128)(2,1)S(1)}, u32[]{:S(2)}, u32[]{:S(2)}) collective-permute-start(bf16[2,2,512,256]{3,2,1,0:T(8,128)(2,1)} %get-tuple-element.28.tile), channel_id=1, source_target_pairs={{0,15},{1,0},{2,1},{3,2},{4,3},{5,4},{6,5},{7,6},{8,7},{9,8},{10,9... | collective-permute-start | bytes 3145736 | tf_op jit(solution)/shard_map/ppermute | solution.py:414
  22.9 19.8 %collective-permute-start.1 = (bf16[2,2,512,128]{3,2,1,0:T(8,128)(2,1)}, bf16[2,2,512,128]{3,2,1,0:T(8,128)(2,1)}, u32[]{:S(2)}, u32[]{:S(2)}) collective-permute-start(bf16[2,2,512,128]{3,2,1,0:T(8,128)(2,1)} %get-tuple-element.29), channel_id=1, source_target_pairs={{0,1},{1,2},{2,3},{3,4},{4,5},{5,6},{6,7},{7,8},{8,9},{9,10},{10,1... | collective-permute-start | bytes 1572872 | tf_op jit(solution)/shard_map/ppermute | solution.py:415
  30.4 40.8 %all-to-all-start.1 = ((bf16[16,256,256]{2,1,0:T(8,128)(2,1)}), bf16[16,256,256]{2,1,0:T(8,128)(2,1)S(1)}, u32[]{:S(2)}, u32[]{:S(2)}) async-start(bf16[16,256,256]{2,1,0:T(8,128)(2,1)} %shard_map.117), calls=%async_computation.1 | async-start | bytes 4194304 | tf_op jit(solution)/shard_map/all_to_all | solution.py:434
  54.6 1.1 copy-start.8
  71.3 1.3 copy-start
  92.9 3.8 %copy-start.7 = (bf16[2,2,512,256]{3,2,1,0:T(8,128)(2,1)S(1)}, bf16[2,2,512,256]{3,2,1,0:T(8,128)(2,1)}, u32[]{:S(2)}) copy-start(bf16[2,2,512,256]{3,2,1,0:T(8,128)(2,1)} %get-tuple-element.37) | copy-start | bytes 3145732
  92.9 20.4 %all-to-all-start.2 = ((bf16[16,128,256]{2,1,0:T(8,128)(2,1)}), bf16[16,128,256]{2,1,0:T(8,128)(2,1)S(1)}, u32[]{:S(2)}, u32[]{:S(2)}) async-start(bf16[16,128,256]{2,1,0:T(8,128)(2,1)} %bitcast.10), calls=%async_computation.2 | async-start | bytes 2097152 | tf_op jit(solution)/shard_map/all_to_all | solution.py:503
  96.7 48.6 %collective-permute-start.2 = (bf16[2,2,512,256]{3,2,1,0:T(8,128)(2,1)S(1)}, bf16[2,2,512,256]{3,2,1,0:T(8,128)(2,1)S(1)}, u32[]{:S(2)}, u32[]{:S(2)}) collective-permute-start(bf16[2,2,512,256]{3,2,1,0:T(8,128)(2,1)S(1)} %copy-done.7), channel_id=1, source_target_pairs={{0,1},{1,2},{2,3},{3,4},{4,5},{5,6},{6,7},{7,8},{8,9},{9,10},{10,1... | collective-permute-start | bytes 3145736 | tf_op jit(solution)/shard_map/ppermute | solution.py:500
  114.3 24.0 %all-to-all-start.3 = ((bf16[8,128,256]{2,1,0:T(8,128)(2,1)}), bf16[8,128,256]{2,1,0:T(8,128)(2,1)S(1)}, u32[]{:S(2)}, u32[]{:S(2)}) async-start(bf16[8,128,256]{2,1,0:T(8,128)(2,1)} %broadcast_in_dim.6), calls=%async_computation.3 | async-start | bytes 1048576 | tf_op jit(solution)/shard_map/all_to_all | solution.py:508
  127.2 18.2 %collective-permute-start.3 = (bf16[2,2,512,128]{3,2,1,0:T(8,128)(2,1)}, bf16[2,2,512,128]{3,2,1,0:T(8,128)(2,1)S(1)}, u32[]{:S(2)}, u32[]{:S(2)}) collective-permute-start(bf16[2,2,512,128]{3,2,1,0:T(8,128)(2,1)} %get-tuple-element.38), channel_id=1, source_target_pairs={{0,15},{1,0},{2,1},{3,2},{4,3},{5,4},{6,5},{7,6},{8,7},{9,8},{10,9... | collective-permute-start | bytes 1572872 | tf_op jit(solution)/shard_map/ppermute | solution.py:501
  145.3 0.8 copy-start.4
  146.1 1.0 copy-start.2
  148.2 8.5 %copy-start.1 = (f32[2,2,512,256]{3,2,1,0:T(8,128)S(1)}, f32[2,2,512,256]{3,2,1,0:T(8,128)}, u32[]{:S(2)}) copy-start(f32[2,2,512,256]{3,2,1,0:T(8,128)} %get-tuple-element.35) | copy-start | bytes 6291460
  148.2 21.9 %all-to-all-start.4 = ((bf16[16,128,256]{2,1,0:T(8,128)(2,1)}), bf16[16,128,256]{2,1,0:T(8,128)(2,1)S(1)}, u32[]{:S(2)}, u32[]{:S(2)}) async-start(bf16[16,128,256]{2,1,0:T(8,128)(2,1)} %broadcast_in_dim.8), calls=%async_computation.4 | async-start | bytes 2097152 | tf_op jit(solution)/shard_map/all_to_all | solution.py:513
  155.4 1.4 copy-start.3

commit v2 on v1

--- a/solution.py
+++ b/solution.py
@@ -11,7 +11,7 @@
 SIZE = 256
 HALF = 128
 MODES = 4
-CHUNK = 32
+CHUNK = 16
 SLOTS = 8
 BF16 = jnp.bfloat16
 F32 = jnp.float32
@@ -22,9 +22,19 @@
     phase = 2.0 * np.pi * ((index[:, None] * index[None, :]) % SIZE) / SIZE
     real = np.cos(phase) / math.sqrt(SIZE)
     imag = -np.sin(phase) / math.sqrt(SIZE)
-    left = np.block([[real, -imag], [imag, real]])
-    right = np.block([[real, imag], [-imag, real]])
-    return jnp.asarray(left, F32).astype(BF16), jnp.asarray(right, F32).astype(BF16)
+    halves = []
+    for first in range(2):
+        re, im = real[first::2, :HALF], imag[first::2, :HALF]
+        halves.append(np.block([[re, -im], [im, re]]))
+    both = np.stack(halves + [half.T for half in halves])
+    return jnp.asarray(both, F32).astype(BF16)
+
+
+def sorter():
+    index = np.arange(SIZE)
+    place = index // 2 + HALF * (index % 2)
+    sort = place[:, None] == index[None, :]
+    return jnp.asarray(np.stack([sort, sort.T]), BF16)
 
 
 def describe_kernel(info, notes):
@@ -64,9 +74,9 @@
             notes[t * SLOTS + n] = 0
 
 
-def assign_kernel(me, notes, codes, homes, loads):
+def assign_kernel(me, notes, packed, codes, slots, loads, homes, sems):
     tiles = codes.shape[0]
-    scans = homes.shape[0]
+    scans = packed.shape[0]
     for t in range(tiles):
         loads[t] = 0
 
@@ -97,6 +107,16 @@
 
         codes[source] = code
 
+    def each(act):
+        for n in range(scans):
+
+            @pl.when(homes[n] >= 0)
+            def _():
+                act(pltpu.make_async_copy(packed.at[n], slots.at[homes[n]], sems.at[n]))
+
+    each(lambda copy: copy.start())
+    each(lambda copy: copy.wait())
+
 
 def cast_kernel(odd, obj, tile_low, half):
     side = pl.multiple_of((1 - odd[0]) * HALF, HALF)
@@ -104,12 +124,15 @@
     half[...] = obj[:, :, :, pl.ds(side, HALF)].astype(BF16)
 
 
-def pack_kernel(homes, measured, slots):
-    for n in range(measured.shape[0]):
-
-        @pl.when(homes[n] >= 0)
+def sort_kernel(info, measured, sort, packed):
+    scans = measured.shape[0]
+    for n in range(scans):
+
+        @pl.when(n < info[4 * scans])
         def _():
-            slots[homes[n]] = measured[n].astype(BF16)
+            rows = jnp.dot(sort[1], measured[n].astype(BF16), preferred_element_type=F32)
+            both = jnp.dot(rows.astype(BF16), sort[0], preferred_element_type=F32)
+            packed[n] = both.astype(BF16)
 
 
 def banded(taps, row, shift):
@@ -141,22 +164,98 @@
 CHUNKS = [slice(at, at + CHUNK) for at in range(0, SIZE, CHUNK)]
 
 
+def in_turn(*stages):
+    for step in range(MODES + len(stages) - 1):
+        for place, stage in enumerate(stages):
+            if 0 <= step - place < MODES:
+                stage(step - place)
+
+
+def rows_of(m):
+    return slice(m * SIZE, (m + 1) * SIZE)
+
+
 def left_stage(table, rows_in, cols_in):
-    both = jnp.dot(table, rows_in[...], preferred_element_type=F32).astype(BF16)
-    for m in range(MODES):
-        rows, cols = slice(m * SIZE, (m + 1) * SIZE), slice(m * SIZE, (m + 1) * SIZE)
-        cols_in[rows, :SIZE] = both[:SIZE, cols]
-        cols_in[rows, SIZE:] = both[SIZE:, cols]
+    def stage(m):
+        both = jnp.dot(table, rows_in[m], preferred_element_type=F32)
+        cols_in[rows_of(m), :SIZE] = both[:SIZE].astype(BF16)
+        cols_in[rows_of(m), SIZE:] = both[SIZE:].astype(BF16)
+
+    return stage
 
 
 def right_stage(table, cols_in, out):
-    out[...] = jnp.dot(cols_in[...], table, preferred_element_type=F32)
+    def stage(m):
+        out[rows_of(m), :] = jnp.dot(cols_in[rows_of(m), :], table, preferred_element_type=F32)
+
+    return stage
 
 
 def put_rows(rows_in, m, at, real, imag):
-    cols = slice(m * SIZE, (m + 1) * SIZE)
-    rows_in[at.start : at.stop, cols] = real.astype(BF16)
-    rows_in[SIZE + at.start : SIZE + at.stop, cols] = imag.astype(BF16)
+    rows_in[m, at.start : at.stop, :] = real.astype(BF16)
+    rows_in[m, SIZE + at.start : SIZE + at.stop, :] = imag.astype(BF16)
+
+
+def put_halves(rows_in, m, at, first, second):
+    for place, part in enumerate(first + second):
+        low = place * HALF + at.start
+        rows_in[m, low : low + CHUNK, :] = part.astype(BF16)
+
+
+def dft_left(dft, rows_in, cols_in):
+    def stage(m):
+        for first in range(2):
+            part = slice(first * SIZE, (first + 1) * SIZE)
+            both = jnp.dot(dft[first], rows_in[m, part, :], preferred_element_type=F32)
+            rows = slice(m * SIZE + first * HALF, m * SIZE + (first + 1) * HALF)
+            for k in range(2):
+                here = both[k * HALF : (k + 1) * HALF]
+                low, high = here[:, :HALF], here[:, HALF:]
+                cols_in[rows, k * HALF : (k + 1) * HALF] = (low + high).astype(BF16)
+                cols_in[rows, SIZE + k * HALF : SIZE + (k + 1) * HALF] = (low - high).astype(BF16)
+
+    return stage
+
+
+def dft_right(dft, cols_in, out):
+    def stage(m):
+        for first in range(2):
+            part = slice(first * SIZE, (first + 1) * SIZE)
+            both = jnp.dot(cols_in[rows_of(m), part], dft[2 + first], preferred_element_type=F32)
+            for k in range(2):
+                low = k * SIZE + first * HALF
+                out[rows_of(m), low : low + HALF] = both[:, k * HALF : (k + 1) * HALF]
+
+    return stage
+
+
+def inverse_left(dft, rows_in, cols_in):
+    def stage(m):
+        even = jnp.dot(dft[2], rows_in[m, :SIZE, :], preferred_element_type=F32)
+        odd = jnp.dot(dft[3], rows_in[m, SIZE:, :], preferred_element_type=F32)
+        for k in range(2):
+            part = slice(k * HALF, (k + 1) * HALF)
+            sums = (even[part] + odd[part]).astype(BF16)
+            gaps = (even[part] - odd[part]).astype(BF16)
+            for side in range(2):
+                here = slice(side * HALF, (side + 1) * HALF)
+                low = side * SIZE + k * HALF
+                cols_in[m * SIZE : m * SIZE + HALF, low : low + HALF] = sums[:, here]
+                cols_in[m * SIZE + HALF : (m + 1) * SIZE, low : low + HALF] = gaps[:, here]
+
+    return stage
+
+
+def inverse_right(dft, cols_in, out):
+    def stage(m):
+        even = jnp.dot(cols_in[rows_of(m), :SIZE], dft[0], preferred_element_type=F32)
+        odd = jnp.dot(cols_in[rows_of(m), SIZE:], dft[1], preferred_element_type=F32)
+        for k in range(2):
+            part = slice(k * HALF, (k + 1) * HALF)
+            out[rows_of(m), k * SIZE : k * SIZE + HALF] = even[:, part] + odd[:, part]
+            out[rows_of(m), k * SIZE + HALF : (k + 1) * SIZE] = even[:, part] - odd[:, part]
+
+    return stage
 
 
 def pair(ref, m, at):
@@ -192,7 +291,7 @@
 
 
 def forward_kernel(
-    odd, codes, full, tile, half, probe, taps, dft_left, dft_right,
+    odd, codes, full, tile, half, probe, taps, dft,
     moved_all, far_all, root_all, patch_all,
     ext, tables, rows_in, cols_in, moved_two, far_two, root_two, patch_two, order, sems,
 ):
@@ -225,20 +324,32 @@
                 for side in range(2):
                     low = part * SIZE + side * HALF
                     patch[s, :, low : low + HALF] = ext[column + side, s, part, pl.ds(start, SIZE), :]
-        for at in CHUNKS:
-            o_re, o_im = pair_of(patch, 0, at)
-            for m in range(MODES):
+
+        def wave(m):
+            for at in CHUNKS:
+                o_re, o_im = pair_of(patch, 0, at)
                 p_re, p_im = probe[m, 0, at, :].astype(F32), probe[m, 1, at, :].astype(F32)
                 put_rows(rows_in, m, at, p_re * o_re - p_im * o_im, p_re * o_im + p_im * o_re)
-        left_stage(tables[0], rows_in, cols_in)
-        right_stage(tables[1], cols_in, moved)
-        for at in CHUNKS:
-            o_re, o_im = pair_of(patch, 1, at)
-            for m in range(MODES):
+
+        def exit_wave(m):
+            for at in CHUNKS[: len(CHUNKS) // 2]:
+                down = slice(at.start + HALF, at.stop + HALF)
+                o_re, o_im = pair_of(patch, 1, at)
+                q_re, q_im = pair_of(patch, 1, down)
                 v_re, v_im = pair(moved, m, at)
-                put_rows(rows_in, m, at, v_re * o_re - v_im * o_im, v_re * o_im + v_im * o_re)
-        left_stage(dft_left[...], rows_in, cols_in)
-        right_stage(dft_right[...], cols_in, far)
+                w_re, w_im = pair(moved, m, down)
+                a_re, a_im = v_re * o_re - v_im * o_im, v_re * o_im + v_im * o_re
+                b_re, b_im = w_re * q_re - w_im * q_im, w_re * q_im + w_im * q_re
+                put_halves(rows_in, m, at, (a_re + b_re, a_im + b_im), (a_re - b_re, a_im - b_im))
+
+        in_turn(
+            wave,
+            left_stage(tables[0], rows_in, cols_in),
+            right_stage(tables[1], cols_in, moved),
+            exit_wave,
+            dft_left(dft, rows_in, cols_in),
+            dft_right(dft, cols_in, far),
+        )
         for at in CHUNKS:
             power = jnp.ones((CHUNK, SIZE), F32)
             for m in range(MODES):
@@ -257,11 +368,11 @@
 
 
 def backward_kernel(
-    odd, codes, dft_left, dft_right, taps, probe_all,
+    odd, codes, dft, taps, probe_all,
     moved_all, far_all, root_all, patch_all, slots_all,
     own_grad, full_grad, half_grad, probe_grad,
     rows_in, cols_in, moved_two, far_two, root_two, patch_two, slots_two,
-    probe, adjoints, acc, probe_acc, order, sems, once, ends,
+    factor, probe, adjoints, acc, probe_acc, order, sems, once, ends,
 ):
     found = live_list(codes, order)
     wholes = (far_all, slots_all, root_all, moved_all, patch_all)
@@ -304,13 +415,22 @@
         column, start = place_of(codes[order[i]])
         for copy in copies(i):
             copy.wait()
+
+        def scaled(m):
+            for at in CHUNKS[: len(CHUNKS) // 2]:
+                down = slice(at.start + HALF, at.stop + HALF)
+                f_re, f_im = pair(far, m, at)
+                g_re, g_im = pair(far, m, down)
+                top, low = factor[at, :], factor[down, :]
+                put_halves(rows_in, m, at, (top * f_re, top * f_im), (low * g_re, low * g_im))
+
         for at in CHUNKS:
-            factor = 1.0 - slot[at, :].astype(F32) * root[at, :]
-            for m in range(MODES):
-                f_re, f_im = pair(far, m, at)
-                put_rows(rows_in, m, at, factor * f_re, factor * f_im)
-        left_stage(dft_right[...], rows_in, cols_in)
-        right_stage(dft_left[...], cols_in, far)
+            factor[at, :] = 1.0 - slot[at, :].astype(F32) * root[at, :]
+        in_turn(
+            scaled,
+            inverse_left(dft, rows_in, cols_in),
+            inverse_right(dft, cols_in, far),
+        )
         for at in CHUNKS:
             o_re, o_im = pair_of(patch, 1, at)
             g_re = jnp.zeros((CHUNK, SIZE), F32)
@@ -323,8 +443,10 @@
                 put_rows(rows_in, m, at, o_re * a_re + o_im * a_im, o_re * a_im - o_im * a_re)
             add_piece(1, at, column, start, g_re, g_im)
 
-        left_stage(adjoints[0], rows_in, cols_in)
-        right_stage(adjoints[1], cols_in, moved)
+        in_turn(
+            left_stage(adjoints[0], rows_in, cols_in),
+            right_stage(adjoints[1], cols_in, moved),
+        )
 
         @pl.when(i == 0)
         def _():
@@ -379,18 +501,17 @@
     tile_shape = (2, 2, band, SIZE)
     scans = measured.shape[0]
     odd = (lax.axis_index("row") % 2).reshape(1)
-    info = [scan_corner.reshape(-1), correlation.reshape(-1), scan_count.reshape(-1), odd]
-    notes = pl.pallas_call(
-        describe_kernel,
-        out_shape=jax.ShapeDtypeStruct((cols * SLOTS,), jnp.int32),
-        in_specs=scalars(1),
-        out_specs=pl.BlockSpec(memory_space=pltpu.SMEM),
-        compiler_params=limit,
-    )(jnp.concatenate(info))
-    notes, object_slices = lax.optimization_barrier((notes, object_slices))
-    row_notes = lax.all_to_all(
-        notes.reshape(cols, SLOTS), "col", split_axis=0, concat_axis=0, tiled=True
-    )
+    def anywhere(count):
+        return [pl.BlockSpec(memory_space=pl.ANY) for _ in range(count)]
+
+    def ring(step):
+        pairs = []
+        for r in range(rows):
+            way = step if r % 2 == 0 else -step
+            pairs += [(r * cols + c, r * cols + (c + way) % cols) for c in range(cols)]
+        return pairs
+
+    both = ("row", "col")
     tile_low, half = pl.pallas_call(
         cast_kernel,
         out_shape=[
@@ -401,51 +522,55 @@
         out_specs=whole(2),
         compiler_params=limit,
     )(odd, object_slices)
-    row_notes, tile_low, half = lax.optimization_barrier((row_notes, tile_low, half))
-
-    def ring(step):
-        pairs = []
-        for r in range(rows):
-            way = step if r % 2 == 0 else -step
-            pairs += [(r * cols + c, r * cols + (c + way) % cols) for c in range(cols)]
-        return pairs
-
-    both = ("row", "col")
     full = lax.ppermute(tile_low, both, ring(-1))
     half = lax.ppermute(half, both, ring(1))
-    codes, homes = pl.pallas_call(
+
+    info = [scan_corner.reshape(-1), correlation.reshape(-1), scan_count.reshape(-1), odd]
+    info = jnp.concatenate(info)
+    notes = pl.pallas_call(
+        describe_kernel,
+        out_shape=jax.ShapeDtypeStruct((cols * SLOTS,), jnp.int32),
+        in_specs=scalars(1),
+        out_specs=pl.BlockSpec(memory_space=pltpu.SMEM),
+        compiler_params=limit,
+    )(info)
+    row_notes = lax.all_to_all(
+        notes.reshape(cols, SLOTS), "col", split_axis=0, concat_axis=0, tiled=True
+    )
+    packed = pl.pallas_call(
+        sort_kernel,
+        out_shape=jax.ShapeDtypeStruct((scans, SIZE, SIZE), BF16),
+        in_specs=scalars(1) + whole(2),
+        out_specs=pl.BlockSpec(memory_space=pltpu.VMEM),
+        compiler_params=limit,
+    )(info, measured, sorter())
+    codes, slots = pl.pallas_call(
         assign_kernel,
         out_shape=[
             jax.ShapeDtypeStruct((cols,), jnp.int32),
-            jax.ShapeDtypeStruct((scans,), jnp.int32),
+            jax.ShapeDtypeStruct((cols, SIZE, SIZE), BF16),
         ],
-        in_specs=scalars(2),
-        out_specs=scalars(2),
-        scratch_shapes=[pltpu.SMEM((cols,), jnp.int32)],
+        in_specs=scalars(2) + whole(1),
+        out_specs=scalars(1) + anywhere(1),
+        scratch_shapes=[
+            pltpu.SMEM((cols,), jnp.int32),
+            pltpu.SMEM((scans,), jnp.int32),
+            pltpu.SemaphoreType.DMA((scans,)),
+        ],
         compiler_params=limit,
-    )(lax.axis_index("col").reshape(1), row_notes.reshape(cols * SLOTS))
-    slots = pl.pallas_call(
-        pack_kernel,
-        out_shape=jax.ShapeDtypeStruct((cols, SIZE, SIZE), BF16),
-        in_specs=scalars(1) + whole(1),
-        out_specs=pl.BlockSpec(memory_space=pltpu.VMEM),
-        compiler_params=limit,
-    )(homes, measured)
+    )(lax.axis_index("col").reshape(1), row_notes.reshape(cols * SLOTS), packed)
     arrived = lax.all_to_all(slots, "col", split_axis=0, concat_axis=0, tiled=True)
 
     taps = jnp.concatenate([tap_row, tap_col], axis=0)
     taps = jnp.concatenate([taps, taps[:, ::-1]], axis=0)
     taps = jnp.pad(taps, ((0, 0), (0, 2 * SIZE - taps.shape[1])))
-    dft_left, dft_right = dft_tables()
-
-    def anywhere(count):
-        return [pl.BlockSpec(memory_space=pl.ANY) for _ in range(count)]
+    dft = dft_tables()
 
     field_shape = (MODES * SIZE, 2 * SIZE)
     patch_shape = (2, SIZE, 2 * SIZE)
     pair_shape = (2, 2 * SIZE, 2 * SIZE)
     work = [
-        pltpu.VMEM((2 * SIZE, MODES * SIZE), BF16),
+        pltpu.VMEM((MODES, 2 * SIZE, SIZE), BF16),
         pltpu.VMEM(field_shape, BF16),
         pltpu.VMEM((2,) + field_shape, F32),
         pltpu.VMEM((2,) + field_shape, F32),
@@ -461,14 +586,14 @@
             jax.ShapeDtypeStruct((cols, SIZE, SIZE), F32),
             jax.ShapeDtypeStruct((cols,) + patch_shape, BF16),
         ],
-        in_specs=scalars(2) + whole(7),
+        in_specs=scalars(2) + whole(6),
         out_specs=anywhere(4),
         scratch_shapes=[pltpu.VMEM((5,) + part_shape, BF16), pltpu.VMEM(pair_shape, BF16)]
         + work
         + [order, pltpu.SemaphoreType.DMA((2, 4))],
         cost_estimate=pl.CostEstimate(flops=40 * 10**9, bytes_accessed=10**7, transcendentals=0),
         compiler_params=limit,
-    )(odd, codes, full, tile_low, half, probe, taps, dft_left, dft_right)
+    )(odd, codes, full, tile_low, half, probe, taps, dft)
     own_grad, full_grad, half_grad, probe_part = pl.pallas_call(
         backward_kernel,
         out_shape=[
@@ -477,11 +602,12 @@
             jax.ShapeDtypeStruct(part_shape, BF16),
             jax.ShapeDtypeStruct(probe.shape, BF16),
         ],
-        in_specs=scalars(2) + whole(3) + anywhere(6),
+        in_specs=scalars(2) + whole(2) + anywhere(6),
         out_specs=anywhere(1) + whole(3),
         scratch_shapes=work
         + [
             pltpu.VMEM((2, SIZE, SIZE), BF16),
+            pltpu.VMEM((SIZE, SIZE), F32),
             pltpu.VMEM(probe.shape, BF16),
             pltpu.VMEM(pair_shape, BF16),
             pltpu.VMEM((5,) + part_shape, F32),
@@ -493,24 +619,27 @@
         ],
         compiler_params=limit,
     )(
-        odd, codes, dft_left, dft_right, taps, probe,
+        odd, codes, dft, taps, probe,
         moved_all, far_all, root_all, patch_all, arrived,
     )
 
     full_grad = lax.ppermute(full_grad, both, ring(1))
     half_grad = lax.ppermute(half_grad, both, ring(-1))
-    share = MODES * 2 * SIZE // cols
-    mine = lax.all_to_all(
-        probe_part.reshape(cols, share, SIZE), "col", split_axis=0, concat_axis=0, tiled=True
-    )
+    lines = MODES * 2 * SIZE // rows
+    share = lines // cols
+
+    def swap(blocks, axis):
+        return lax.all_to_all(blocks, axis, split_axis=0, concat_axis=0, tiled=True)
+
+    mine = swap(probe_part.reshape(rows, lines, SIZE), "row")
     mine = jnp.sum(mine.astype(F32), axis=0).astype(BF16)
-    mine = jnp.broadcast_to(mine[None], (rows, share, SIZE))
-    mine = lax.all_to_all(mine, "row", split_axis=0, concat_axis=0, tiled=True)
-    scale = 1.0 / math.sqrt(measured.shape[0] * cols * rows)
+    mine = swap(mine.reshape(cols, share, SIZE), "col")
+    scale = 1.0 / math.sqrt(scans * cols * rows)
     mine = (jnp.sum(mine.astype(F32), axis=0) * scale).astype(BF16)
+    mine = swap(jnp.broadcast_to(mine[None], (cols, share, SIZE)), "col")
     mine, full_grad, half_grad = lax.optimization_barrier((mine, full_grad, half_grad))
-    mine = jnp.broadcast_to(mine[None], (cols, share, SIZE))
-    probe_grad = lax.all_to_all(mine, "col", split_axis=0, concat_axis=0, tiled=True)
+    mine = mine.reshape(lines, SIZE)
+    probe_grad = swap(jnp.broadcast_to(mine[None], (rows, lines, SIZE)), "row")
     probe_grad = probe_grad.astype(F32).reshape(probe.shape)
     half_grad = half_grad.astype(F32)
     nothing = jnp.zeros_like(half_grad)

time: 173 us -> 166 us (0.960)
  Pallas kernels: 46.1 us -> 34.3 us
  starting transfers between devices: 52.5 us -> 58.5 us
  local copies, waits for them, and re-layouts: 10 us -> 7.2 us
    all_to_all x1, waiting for transfers between devices: 0.01 us -> 17.5 us  [body(): lax.all_to_all(slots, 'col', split_axis=0, concat_axis=0, tiled=True)]
    ppermute x1, waiting for transfers between devices: 12 us -> 0.01 us  [body(): full = lax.ppermute(tile_low, both, ring(-1))]
    all_to_all x3 -> x4, waiting for transfers between devices: 26.4 us -> 34.8 us  [swap(): return lax.all_to_all(blocks, axis, split_axis=0, concat_axis=0, tiled=True)]
    pallas_call x1, Pallas kernels: 20.3 us -> 12.6 us  [body(): pl.pallas_call(backward_kernel, out_shape=[jax.ShapeDtypeStruct(tile_shap...]
    all_to_all x3 -> x4, starting transfers between devices: 23.9 us -> 31.1 us  [swap(): return lax.all_to_all(blocks, axis, split_axis=0, concat_axis=0, tiled=True)]
    ppermute x1, waiting for transfers between devices: 6.92 us -> 0.49 us  [body(): half_grad = lax.ppermute(half_grad, both, ring(-1))]
    pallas_call x1, Pallas kernels: 15.5 us -> 9.3 us  [body(): pl.pallas_call(forward_kernel, out_shape=[jax.ShapeDtypeStruct((cols,) +...]
    ppermute x1, starting transfers between devices: 11.1 us -> 5.25 us  [body(): half_grad = lax.ppermute(half_grad, both, ring(-1))]
  transfers between devices with their start and end apart: 9 -> 10, of which waited for: 6 -> 7; matrix products, arithmetic and copies ran while one was open for 3% -> 5% of each run, Pallas kernels for 14% -> 11%
where the time goes in v2:
time: 166 us; the launch traced here: 165 us
  starting transfers between devices  58.5 us (35%)
  waiting for transfers between devices  55.9 us (34%)
  Pallas kernels  34.3 us (21%)
  other arithmetic  7.3 us (4%)
  local copies, waits for them, and re-layouts  7.2 us (4%)
    all_to_all x4, waiting for transfers between devices, swap(): return lax.all_to_all(blocks, axis, split_axis=0, concat_axis=0, tiled=True)  34.8 us
    all_to_all x4, starting transfers between devices, swap(): return lax.all_to_all(blocks, axis, split_axis=0, concat_axis=0, tiled=True)  31.1 us
    all_to_all x1, waiting for transfers between devices, body(): lax.all_to_all(slots, 'col', split_axis=0, concat_axis=0, tiled=True)  17.5 us
    pallas_call x1, Pallas kernels, body(): pl.pallas_call(backward_kernel, out_shape=[jax.ShapeDtypeStruct(tile_shap...  12.6 us
    pallas_call x1, Pallas kernels, body(): pl.pallas_call(forward_kernel, out_shape=[jax.ShapeDtypeStruct((cols,) +...  9.3 us
    all_to_all x1, starting transfers between devices, body(): lax.all_to_all(notes.reshape(cols, SLOTS), 'col', split_axis=0, concat_ax...  6.72 us
    all_to_all x1, starting transfers between devices, body(): lax.all_to_all(slots, 'col', split_axis=0, concat_axis=0, tiled=True)  5.89 us
    ppermute x1, starting transfers between devices, body(): full = lax.ppermute(tile_low, both, ring(-1))  5.29 us
  transfers between devices with their start and end apart: 10, of which 7 were waited for; matrix products, arithmetic and copies ran while one was open for 5% of the time, Pallas kernels for 11%

profile of v2, /device:TPU:0, one launch (start us, length us, event | category | flops | bytes accessed | tf_op | source)
XLA Modules:
  0.0 164.7 jit_solution(12854057438245710868)
XLA Ops:
  0.7 2.9 %shard_map.116 = (bf16[2,2,512,256]{3,2,1,0:T(8,128)(2,1)}, bf16[2,2,512,128]{3,2,1,0:T(8,128)(2,1)}) custom-call(s32[1]{0:T(128)} %bitcast.odd, f32[2,2,512,256]{3,2,1,0:T(8,128)} %obj.1), custom_call_target="tpu_custom_call" | custom-call | tf_op jit(solution)/shard_map/pallas_call | solution.py:515
  3.6 5.3 %collective-permute-start = (bf16[2,2,512,256]{3,2,1,0:T(8,128)(2,1)}, bf16[2,2,512,256]{3,2,1,0:T(8,128)(2,1)S(1)}, u32[]{:S(2)}, u32[]{:S(2)}) collective-permute-start(bf16[2,2,512,256]{3,2,1,0:T(8,128)(2,1)} %get-tuple-element.18.tile), channel_id=1, source_target_pairs={{0,15},{1,0},{2,1},{3,2},{4,3},{5,4},{6,5},{7,6},{8,7},{9,8},{10,9... | collective-permute-start | bytes 3145736 | tf_op jit(solution)/shard_map/ppermute | solution.py:525
  8.9 0.0 collective-permute-start.1
  8.9 0.0 copy-done.7
  8.9 0.1 copy.19
  9.0 0.1 reshape.46
  9.1 0.1 copy.20
  9.2 0.1 reshape.47
  9.9 0.7 pad_add_fusion.info
  10.6 1.5 shard_map.113
  12.1 1.4 all_to_all.21
  13.4 6.7 %all-to-all-start = ((s32[16,1,8]{2,1,0:T(1,128)}), s32[16,1,8]{2,1,0:T(1,128)S(1)}, u32[]{:S(2)}, u32[]{:S(2)}) async-start(s32[16,1,8]{2,1,0:T(1,128)} %bitcast.3), calls=%async_computation | async-start | bytes 16384 | tf_op jit(solution)/shard_map/all_to_all | solution.py:537
  20.2 0.1 rev.3
  20.3 0.6 select_maximum_fusion.taps
  20.9 3.7 %shard_map.114.packed = bf16[6,256,256]{2,1,0:T(8,128)(2,1)} custom-call(s32[26]{0:T(128)} %pad_add_fusion.info, f32[6,256,256]{2,1,0:T(8,128)} %measured.1, bf16[2,256,256]{2,1,0:T(8,128)(2,1)} %constant.36.clone.sort), custom_call_target="tpu_custom_call" | custom-call | tf_op jit(solution)/shard_map/pallas_call | solution.py:540
  24.6 3.1 %all-to-all-done = s32[16,1,8]{2,1,0:T(1,128)S(1)} async-done(((s32[16,1,8]{2,1,0:T(1,128)}), s32[16,1,8]{2,1,0:T(1,128)S(1)}, u32[]{:S(2)}, u32[]{:S(2)}) %all-to-all-start) | async-done | bytes 544 | tf_op jit(solution)/shard_map/all_to_all | solution.py:537
  27.6 0.5 broadcast.18
  28.2 0.7 reduce.4
  28.8 0.7 reshape.49.notes
  29.5 4.3 %shard_map.115 = (s32[16]{0:T(128)}, bf16[16,256,256]{2,1,0:T(8,128)(2,1)}) custom-call(s32[1]{0:T(128)} %bitcast.1.me, s32[128]{0:T(128)} %reshape.49.notes, bf16[6,256,256]{2,1,0:T(8,128)(2,1)} %shard_map.114.packed), custom_call_target="tpu_custom_call" | custom-call | tf_op jit(solution)/shard_map/pallas_call | solution.py:547
  33.9 5.9 %all-to-all-start.1 = ((bf16[16,256,256]{2,1,0:T(8,128)(2,1)}), bf16[16,256,256]{2,1,0:T(8,128)(2,1)S(1)}, u32[]{:S(2)}, u32[]{:S(2)}) async-start(bf16[16,256,256]{2,1,0:T(8,128)(2,1)} %get-tuple-element.24), calls=%async_computation.1 | async-start | bytes 4194304 | tf_op jit(solution)/shard_map/all_to_all | solution.py:562
  39.8 0.0 collective-permute-done.1.half
  39.8 0.0 collective-permute-done.full
  39.8 1.0 copy-done.9
  40.8 9.3 %shard_map.117 = (f32[16,1024,512]{2,1,0:T(8,128)}, f32[16,1024,512]{2,1,0:T(8,128)}, f32[16,256,256]{2,1,0:T(8,128)}, bf16[16,2,256,512]{3,2,1,0:T(8,128)(2,1)}) custom-call(s32[1]{0:T(128)} %bitcast.odd, s32[16]{0:T(128)} %get-tuple-element.17.codes, bf16[2,2,512,256]{3,2,1,0:T(8,128)(2,1)} %copy-done.9, bf16[2,2,512,256]{3,2,1,0:T(8,128)(2,1)} %get-tuple-element.18.tile, ...), custom_call_target="tpu_custom_call" | custom-call | flops 40000000000 | bytes 10000000 | tf_op jit(solution)/shard_map/pallas_call | solution.py:581
  50.1 17.5 %all-to-all-done.1.slots_all = bf16[16,256,256]{2,1,0:T(8,128)(2,1)S(1)} async-done(((bf16[16,256,256]{2,1,0:T(8,128)(2,1)}), bf16[16,256,256]{2,1,0:T(8,128)(2,1)S(1)}, u32[]{:S(2)}, u32[]{:S(2)}) %all-to-all-start.1) | async-done | bytes 2097184 | tf_op jit(solution)/shard_map/all_to_all | solution.py:562
  67.6 1.3 copy-done
  69.0 12.6 %shard_map.118 = (f32[2,2,512,256]{3,2,1,0:T(8,128)}, bf16[2,2,512,256]{3,2,1,0:T(8,128)(2,1)}, bf16[2,2,512,128]{3,2,1,0:T(8,128)(2,1)}, bf16[4,2,256,256]{3,2,1,0:T(8,128)(2,1)}) custom-call(s32[1]{0:T(128)} %bitcast.odd, s32[16]{0:T(128)} %get-tuple-element.17.codes, bf16[4,256,256]{2,1,0:T(8,128)(2,1)} %constant.44.dft, ...), custom_call_target="tpu_custom_call" | custom-call | tf_op jit(solution)/shard_map/pallas_call | solution.py:597
  81.6 11.2 %all-to-all-start.2 = ((bf16[8,256,256]{2,1,0:T(8,128)(2,1)}), bf16[8,256,256]{2,1,0:T(8,128)(2,1)S(1)}, u32[]{:S(2)}, u32[]{:S(2)}) async-start(bf16[8,256,256]{2,1,0:T(8,128)(2,1)} %bitcast.11), calls=%async_computation.2 | async-start | bytes 2097152 | tf_op jit(solution)/shard_map/all_to_all | solution.py:632
  92.8 4.3 %collective-permute-start.2 = (bf16[2,2,512,256]{3,2,1,0:T(8,128)(2,1)S(1)}, bf16[2,2,512,256]{3,2,1,0:T(8,128)(2,1)S(1)}, u32[]{:S(2)}, u32[]{:S(2)}) collective-permute-start(bf16[2,2,512,256]{3,2,1,0:T(8,128)(2,1)S(1)} %copy-done.10), channel_id=1, source_target_pairs={{0,1},{1,2},{2,3},{3,4},{4,5},{5,6},{6,7},{7,8},{8,9},{9,10},{10,1... | collective-permute-start | bytes 3145736 | tf_op jit(solution)/shard_map/ppermute | solution.py:626
  97.0 11.7 %all-to-all-done.2 = bf16[8,256,256]{2,1,0:T(8,128)(2,1)S(1)} async-done(((bf16[8,256,256]{2,1,0:T(8,128)(2,1)}), bf16[8,256,256]{2,1,0:T(8,128)(2,1)S(1)}, u32[]{:S(2)}, u32[]{:S(2)}) %all-to-all-start.2) | async-done | bytes 1048608 | tf_op jit(solution)/shard_map/all_to_all | solution.py:632
  108.7 0.8 reduce_sum.21
  109.5 12.7 %all-to-all-start.3 = ((bf16[16,16,256]{2,1,0:T(8,128)(2,1)}), bf16[16,16,256]{2,1,0:T(8,128)(2,1)S(1)}, u32[]{:S(2)}, u32[]{:S(2)}) async-start(bf16[16,16,256]{2,1,0:T(8,128)(2,1)} %bitcast.5), calls=%async_computation.3 | async-start | bytes 262144 | tf_op jit(solution)/shard_map/all_to_all | solution.py:632
  122.2 5.3 %collective-permute-start.3 = (bf16[2,2,512,128]{3,2,1,0:T(8,128)(2,1)}, bf16[2,2,512,128]{3,2,1,0:T(8,128)(2,1)S(1)}, u32[]{:S(2)}, u32[]{:S(2)}) collective-permute-start(bf16[2,2,512,128]{3,2,1,0:T(8,128)(2,1)} %get-tuple-element.28), channel_id=1, source_target_pairs={{0,15},{1,0},{2,1},{3,2},{4,3},{5,4},{6,5},{7,6},{8,7},{9,8},{10,9... | collective-permute-start | bytes 1572872 | tf_op jit(solution)/shard_map/ppermute | solution.py:627
  127.5 3.0 %all-to-all-done.3 = bf16[16,16,256]{2,1,0:T(8,128)(2,1)S(1)} async-done(((bf16[16,16,256]{2,1,0:T(8,128)(2,1)}), bf16[16,16,256]{2,1,0:T(8,128)(2,1)S(1)}, u32[]{:S(2)}, u32[]{:S(2)}) %all-to-all-start.3) | async-done | bytes 131104 | tf_op jit(solution)/shard_map/all_to_all | solution.py:632
  130.6 0.7 broadcast_in_dim.16
  131.2 3.5 %all-to-all-start.4 = ((bf16[16,16,256]{2,1,0:T(8,128)(2,1)}), bf16[16,16,256]{2,1,0:T(8,128)(2,1)S(1)}, u32[]{:S(2)}, u32[]{:S(2)}) async-start(bf16[16,16,256]{2,1,0:T(8,128)(2,1)} %broadcast_in_dim.16), calls=%async_computation.4 | async-start | bytes 262144 | tf_op jit(solution)/shard_map/all_to_all | solution.py:632
  134.7 0.5 collective-permute-done.3
  135.2 0.0 collective-permute-done.2
  135.2 7.3 %all-to-all-done.4 = bf16[16,16,256]{2,1,0:T(8,128)(2,1)S(1)} async-done(((bf16[16,16,256]{2,1,0:T(8,128)(2,1)}), bf16[16,16,256]{2,1,0:T(8,128)(2,1)S(1)}, u32[]{:S(2)}, u32[]{:S(2)}) %all-to-all-start.4) | async-done | bytes 131104 | tf_op jit(solution)/shard_map/all_to_all | solution.py:632
  142.5 1.1 broadcast_in_dim.19
  143.6 3.7 %all-to-all-start.5 = ((bf16[8,256,256]{2,1,0:T(8,128)(2,1)}), bf16[8,256,256]{2,1,0:T(8,128)(2,1)S(1)}, u32[]{:S(2)}, u32[]{:S(2)}) async-start(bf16[8,256,256]{2,1,0:T(8,128)(2,1)} %broadcast_in_dim.19), calls=%async_computation.5 | async-start | bytes 2097152 | tf_op jit(solution)/shard_map/all_to_all | solution.py:632
  147.3 0.0 copy-start.3
  147.3 1.3 convert_select_fusion.1
  148.6 0.1 copy-done.3
  148.7 1.7 %maximum_add_fusion = f32[2,2,512,256]{3,2,1,0:T(8,128)} fusion(f32[2,2,512,128]{3,2,1,0:T(8,128)S(1)} %get-tuple-element.33, f32[2,2,512,128]{3,2,1,0:T(8,128)S(1)} %get-tuple-element.32, f32[2,2,512,256]{3,2,1,0:T(8,128)S(1)} %copy-done.1, bf16[2,2,512,256]{3,2,1,0:T(8,128)(2,1)S(1)} %copy-done.3), kind=kLoop, calls=%fused_computation | loop fusion | flops 2097152 | bytes 7340032 | tf_op jit(solution)/shard_map/add | solution.py:648
  150.4 12.8 %all-to-all-done.5 = bf16[8,256,256]{2,1,0:T(8,128)(2,1)S(1)} async-done(((bf16[8,256,256]{2,1,0:T(8,128)(2,1)}), bf16[8,256,256]{2,1,0:T(8,128)(2,1)S(1)}, u32[]{:S(2)}, u32[]{:S(2)}) %all-to-all-start.5) | async-done | bytes 1048608 | tf_op jit(solution)/shard_map/all_to_all | solution.py:632
  163.2 1.5 convert.2
  (20 shorter events, 0.1 us)
Async XLA Ops:
  0.6 8.3 %copy-start.7 = (s32[6,2]{0,1:T(2,128)S(1)}, s32[6,2]{0,1:T(2,128)}, u32[]{:S(2)}) copy-start(s32[6,2]{0,1:T(2,128)} %param.15) | copy-start | bytes 148
  0.6 8.4 %copy-start.8 = (s32[6,2]{0,1:T(2,128)S(1)}, s32[6,2]{0,1:T(2,128)}, u32[]{:S(2)}) copy-start(s32[6,2]{0,1:T(2,128)} %param.16) | copy-start | bytes 148
  0.7 19.5 %copy-start.6 = (f32[2,64]{1,0:T(2,128)S(1)}, f32[2,64]{1,0:T(2,128)}, u32[]{:S(2)}) copy-start(f32[2,64]{1,0:T(2,128)} %param.13) | copy-start | bytes 1540
  0.7 19.5 %copy-start.5 = (f32[2,64]{1,0:T(2,128)S(1)}, f32[2,64]{1,0:T(2,128)}, u32[]{:S(2)}) copy-start(f32[2,64]{1,0:T(2,128)} %param.14) | copy-start | bytes 1540
  3.6 36.2 %collective-permute-start = (bf16[2,2,512,256]{3,2,1,0:T(8,128)(2,1)}, bf16[2,2,512,256]{3,2,1,0:T(8,128)(2,1)S(1)}, u32[]{:S(2)}, u32[]{:S(2)}) collective-permute-start(bf16[2,2,512,256]{3,2,1,0:T(8,128)(2,1)} %get-tuple-element.18.tile), channel_id=1, source_target_pairs={{0,15},{1,0},{2,1},{3,2},{4,3},{5,4},{6,5},{7,6},{8,7},{9,8},{10,9... | collective-permute-start | bytes 3145736 | tf_op jit(solution)/shard_map/ppermute | solution.py:525
  8.9 30.9 %collective-permute-start.1 = (bf16[2,2,512,128]{3,2,1,0:T(8,128)(2,1)}, bf16[2,2,512,128]{3,2,1,0:T(8,128)(2,1)}, u32[]{:S(2)}, u32[]{:S(2)}) collective-permute-start(bf16[2,2,512,128]{3,2,1,0:T(8,128)(2,1)} %get-tuple-element.19), channel_id=1, source_target_pairs={{0,1},{1,2},{2,3},{3,4},{4,5},{5,6},{6,7},{7,8},{8,9},{9,10},{10,1... | collective-permute-start | bytes 1572872 | tf_op jit(solution)/shard_map/ppermute | solution.py:526
  13.4 14.2 %all-to-all-start = ((s32[16,1,8]{2,1,0:T(1,128)}), s32[16,1,8]{2,1,0:T(1,128)S(1)}, u32[]{:S(2)}, u32[]{:S(2)}) async-start(s32[16,1,8]{2,1,0:T(1,128)} %bitcast.3), calls=%async_computation | async-start | bytes 16384 | tf_op jit(solution)/shard_map/all_to_all | solution.py:537
  33.9 33.8 %all-to-all-start.1 = ((bf16[16,256,256]{2,1,0:T(8,128)(2,1)}), bf16[16,256,256]{2,1,0:T(8,128)(2,1)S(1)}, u32[]{:S(2)}, u32[]{:S(2)}) async-start(bf16[16,256,256]{2,1,0:T(8,128)(2,1)} %get-tuple-element.24), calls=%async_computation.1 | async-start | bytes 4194304 | tf_op jit(solution)/shard_map/all_to_all | solution.py:562
  39.8 1.1 copy-start.9
  67.6 1.3 copy-start
  81.6 11.2 %copy-start.10 = (bf16[2,2,512,256]{3,2,1,0:T(8,128)(2,1)S(1)}, bf16[2,2,512,256]{3,2,1,0:T(8,128)(2,1)}, u32[]{:S(2)}) copy-start(bf16[2,2,512,256]{3,2,1,0:T(8,128)(2,1)} %get-tuple-element.27) | copy-start | bytes 3145732
  81.6 27.2 %all-to-all-start.2 = ((bf16[8,256,256]{2,1,0:T(8,128)(2,1)}), bf16[8,256,256]{2,1,0:T(8,128)(2,1)S(1)}, u32[]{:S(2)}, u32[]{:S(2)}) async-start(bf16[8,256,256]{2,1,0:T(8,128)(2,1)} %bitcast.11), calls=%async_computation.2 | async-start | bytes 2097152 | tf_op jit(solution)/shard_map/all_to_all | solution.py:632
  92.8 42.5 %collective-permute-start.2 = (bf16[2,2,512,256]{3,2,1,0:T(8,128)(2,1)S(1)}, bf16[2,2,512,256]{3,2,1,0:T(8,128)(2,1)S(1)}, u32[]{:S(2)}, u32[]{:S(2)}) collective-permute-start(bf16[2,2,512,256]{3,2,1,0:T(8,128)(2,1)S(1)} %copy-done.10), channel_id=1, source_target_pairs={{0,1},{1,2},{2,3},{3,4},{4,5},{5,6},{6,7},{7,8},{8,9},{9,10},{10,1... | collective-permute-start | bytes 3145736 | tf_op jit(solution)/shard_map/ppermute | solution.py:626
  109.5 21.0 %all-to-all-start.3 = ((bf16[16,16,256]{2,1,0:T(8,128)(2,1)}), bf16[16,16,256]{2,1,0:T(8,128)(2,1)S(1)}, u32[]{:S(2)}, u32[]{:S(2)}) async-start(bf16[16,16,256]{2,1,0:T(8,128)(2,1)} %bitcast.5), calls=%async_computation.3 | async-start | bytes 262144 | tf_op jit(solution)/shard_map/all_to_all | solution.py:632
  122.2 13.0 %collective-permute-start.3 = (bf16[2,2,512,128]{3,2,1,0:T(8,128)(2,1)}, bf16[2,2,512,128]{3,2,1,0:T(8,128)(2,1)S(1)}, u32[]{:S(2)}, u32[]{:S(2)}) collective-permute-start(bf16[2,2,512,128]{3,2,1,0:T(8,128)(2,1)} %get-tuple-element.28), channel_id=1, source_target_pairs={{0,15},{1,0},{2,1},{3,2},{4,3},{5,4},{6,5},{7,6},{8,7},{9,8},{10,9... | collective-permute-start | bytes 1572872 | tf_op jit(solution)/shard_map/ppermute | solution.py:627
  131.2 11.3 %all-to-all-start.4 = ((bf16[16,16,256]{2,1,0:T(8,128)(2,1)}), bf16[16,16,256]{2,1,0:T(8,128)(2,1)S(1)}, u32[]{:S(2)}, u32[]{:S(2)}) async-start(bf16[16,16,256]{2,1,0:T(8,128)(2,1)} %broadcast_in_dim.16), calls=%async_computation.4 | async-start | bytes 262144 | tf_op jit(solution)/shard_map/all_to_all | solution.py:632
  135.2 7.3 %copy-start.4 = (bf16[2,2,512,128]{3,2,1,0:T(8,128)(2,1)}, bf16[2,2,512,128]{3,2,1,0:T(8,128)(2,1)S(1)}, u32[]{:S(2)}) copy-start(bf16[2,2,512,128]{3,2,1,0:T(8,128)(2,1)S(1)} %collective-permute-done.3) | copy-start | bytes 1572868
  135.2 7.3 %copy-start.2 = (bf16[2,2,512,256]{3,2,1,0:T(8,128)(2,1)}, bf16[2,2,512,256]{3,2,1,0:T(8,128)(2,1)S(1)}, u32[]{:S(2)}) copy-start(bf16[2,2,512,256]{3,2,1,0:T(8,128)(2,1)S(1)} %collective-permute-done.2) | copy-start | bytes 3145732
  143.6 5.0 %copy-start.1 = (f32[2,2,512,256]{3,2,1,0:T(8,128)S(1)}, f32[2,2,512,256]{3,2,1,0:T(8,128)}, u32[]{:S(2)}) copy-start(f32[2,2,512,256]{3,2,1,0:T(8,128)} %get-tuple-element.25) | copy-start | bytes 6291460
  143.6 19.6 %all-to-all-start.5 = ((bf16[8,256,256]{2,1,0:T(8,128)(2,1)}), bf16[8,256,256]{2,1,0:T(8,128)(2,1)S(1)}, u32[]{:S(2)}, u32[]{:S(2)}) async-start(bf16[8,256,256]{2,1,0:T(8,128)(2,1)} %broadcast_in_dim.19), calls=%async_computation.5 | async-start | bytes 2097152 | tf_op jit(solution)/shard_map/all_to_all | solution.py:632
  147.3 1.4 copy-start.3

commit v3 on v2

--- a/solution.py
+++ b/solution.py
@@ -38,7 +38,7 @@
 
 
 def describe_kernel(info, notes):
-    tiles = notes.shape[0] // SLOTS
+    tiles = notes.shape[0]
     scans = (info.shape[0] - 2) // 4
     level = [(info[2 * n] // HALF) % 4 for n in range(scans)]
     straddles = [(info[2 * n + 1] // HALF) % 2 for n in range(scans)]
@@ -68,10 +68,10 @@
         note = live[n] + 2 * free + 4 * owner[n] + 64 * other[n] + 1024 * level[n]
         note = note + 4096 * column + 16384 * moved_column
         for t in range(tiles):
-            notes[t * SLOTS + n] = note
+            notes[t, 0, n] = note
     for t in range(tiles):
         for n in range(scans, SLOTS):
-            notes[t * SLOTS + n] = 0
+            notes[t, 0, n] = 0
 
 
 def assign_kernel(me, notes, packed, codes, slots, loads, homes, sems):
@@ -83,14 +83,14 @@
     @pl.loop(0, tiles)
     def _(source):
         for n in range(scans):
-            note = notes[source * SLOTS + n]
+            note = notes[source, 0, n]
             loads[(note >> 2) & 15] += note & 1
 
     @pl.loop(0, tiles)
     def _(source):
         code = jnp.int32(0)
         for n in range(scans):
-            note = notes[source * SLOTS + n]
+            note = notes[source, 0, n]
             owner, other = (note >> 2) & 15, (note >> 6) & 15
             here, there = loads[owner], loads[other]
             move = ((note >> 1) & 1) * (here > there + 1).astype(jnp.int32)
@@ -298,8 +298,8 @@
     extend(odd[0], full, tile, half, ext)
     put_tables(taps, tables)
     found = live_list(codes, order)
-    wholes = (moved_all, far_all, root_all, patch_all)
-    buffers = (moved_two, far_two, root_two, patch_two)
+    wholes = (root_all, moved_all, far_all, patch_all)
+    buffers = (root_two, moved_two, far_two, patch_two)
 
     def copies(i):
         two = lax.rem(i, 2)
@@ -311,7 +311,7 @@
     @pl.loop(0, found)
     def _(i):
         two = lax.rem(i, 2)
-        moved, far, root, patch = (buffer.at[two] for buffer in buffers)
+        root, moved, far, patch = (buffer.at[two] for buffer in buffers)
 
         @pl.when(i >= 2)
         def _():
@@ -350,14 +350,15 @@
             dft_left(dft, rows_in, cols_in),
             dft_right(dft, cols_in, far),
         )
+        for copy in copies(i)[1:]:
+            copy.start()
         for at in CHUNKS:
             power = jnp.ones((CHUNK, SIZE), F32)
             for m in range(MODES):
                 f_re, f_im = pair(far, m, at)
                 power = power + (f_re * f_re + f_im * f_im)
             root[at, :] = 1.0 / jnp.sqrt(power)
-        for copy in copies(i):
-            copy.start()
+        copies(i)[0].start()
 
     for last in (2, 1):
 
@@ -370,7 +371,7 @@
 def backward_kernel(
     odd, codes, dft, taps, probe_all,
     moved_all, far_all, root_all, patch_all, slots_all,
-    own_grad, full_grad, half_grad, probe_grad,
+    own_grad, full_grad, half_grad, keep, give,
     rows_in, cols_in, moved_two, far_two, root_two, patch_two, slots_two,
     factor, probe, adjoints, acc, probe_acc, order, sems, once, ends,
 ):
@@ -413,7 +414,7 @@
                 copy.start()
 
         column, start = place_of(codes[order[i]])
-        for copy in copies(i):
+        for copy in copies(i)[:3]:
             copy.wait()
 
         def scaled(m):
@@ -431,6 +432,8 @@
             inverse_left(dft, rows_in, cols_in),
             inverse_right(dft, cols_in, far),
         )
+        for copy in copies(i)[3:]:
+            copy.wait()
         for at in CHUNKS:
             o_re, o_im = pair_of(patch, 1, at)
             g_re = jnp.zeros((CHUNK, SIZE), F32)
@@ -478,7 +481,9 @@
     half_grad[...] = acc[4 * odd[0]].astype(BF16)
     full_grad[:, :, :, :HALF] = acc[3 - 3 * odd[0]].astype(BF16)
     full_grad[:, :, :, HALF:] = acc[4 - 3 * odd[0]].astype(BF16)
-    probe_grad[...] = probe_acc[...].astype(BF16)
+    modes = MODES // 2
+    keep[...] = probe_acc[pl.ds(modes * odd[0], modes)].astype(BF16)
+    give[...] = probe_acc[pl.ds(modes * (1 - odd[0]), modes)].astype(BF16)
     for copy in leave:
         copy.wait()
 
@@ -529,14 +534,12 @@
     info = jnp.concatenate(info)
     notes = pl.pallas_call(
         describe_kernel,
-        out_shape=jax.ShapeDtypeStruct((cols * SLOTS,), jnp.int32),
+        out_shape=jax.ShapeDtypeStruct((cols, 1, SLOTS), jnp.int32),
         in_specs=scalars(1),
         out_specs=pl.BlockSpec(memory_space=pltpu.SMEM),
         compiler_params=limit,
     )(info)
-    row_notes = lax.all_to_all(
-        notes.reshape(cols, SLOTS), "col", split_axis=0, concat_axis=0, tiled=True
-    )
+    row_notes = lax.all_to_all(notes, "col", split_axis=0, concat_axis=0, tiled=True)
     packed = pl.pallas_call(
         sort_kernel,
         out_shape=jax.ShapeDtypeStruct((scans, SIZE, SIZE), BF16),
@@ -558,7 +561,7 @@
             pltpu.SemaphoreType.DMA((scans,)),
         ],
         compiler_params=limit,
-    )(lax.axis_index("col").reshape(1), row_notes.reshape(cols * SLOTS), packed)
+    )(lax.axis_index("col").reshape(1), row_notes, packed)
     arrived = lax.all_to_all(slots, "col", split_axis=0, concat_axis=0, tiled=True)
 
     taps = jnp.concatenate([tap_row, tap_col], axis=0)
@@ -594,16 +597,18 @@
         cost_estimate=pl.CostEstimate(flops=40 * 10**9, bytes_accessed=10**7, transcendentals=0),
         compiler_params=limit,
     )(odd, codes, full, tile_low, half, probe, taps, dft)
-    own_grad, full_grad, half_grad, probe_part = pl.pallas_call(
+    half_probe = (MODES // 2,) + probe.shape[1:]
+    own_grad, full_grad, half_grad, keep, give = pl.pallas_call(
         backward_kernel,
         out_shape=[
             jax.ShapeDtypeStruct(tile_shape, F32),
             jax.ShapeDtypeStruct(tile_shape, BF16),
             jax.ShapeDtypeStruct(part_shape, BF16),
-            jax.ShapeDtypeStruct(probe.shape, BF16),
+            jax.ShapeDtypeStruct(half_probe, BF16),
+            jax.ShapeDtypeStruct(half_probe, BF16),
         ],
         in_specs=scalars(2) + whole(2) + anywhere(6),
-        out_specs=anywhere(1) + whole(3),
+        out_specs=anywhere(1) + whole(4),
         scratch_shapes=work
         + [
             pltpu.VMEM((2, SIZE, SIZE), BF16),
@@ -625,22 +630,26 @@
 
     full_grad = lax.ppermute(full_grad, both, ring(1))
     half_grad = lax.ppermute(half_grad, both, ring(-1))
-    lines = MODES * 2 * SIZE // rows
-    share = lines // cols
+    share = MODES * SIZE // cols
+    partner = [(r * cols + c, (r ^ 1) * cols + c) for r in range(rows) for c in range(cols)]
 
     def swap(blocks, axis):
         return lax.all_to_all(blocks, axis, split_axis=0, concat_axis=0, tiled=True)
 
-    mine = swap(probe_part.reshape(rows, lines, SIZE), "row")
+    given = lax.ppermute(give, both, partner)
+    mine = (keep.astype(F32) + given.astype(F32)).astype(BF16)
+    mine = swap(mine.reshape(cols, share, SIZE), "col")
     mine = jnp.sum(mine.astype(F32), axis=0).astype(BF16)
-    mine = swap(mine.reshape(cols, share, SIZE), "col")
+    mine = swap(jnp.broadcast_to(mine[None], (rows, share, SIZE)), "row")
+    same = (jnp.arange(rows) % 2 == odd[0]).astype(F32)
     scale = 1.0 / math.sqrt(scans * cols * rows)
-    mine = (jnp.sum(mine.astype(F32), axis=0) * scale).astype(BF16)
-    mine = swap(jnp.broadcast_to(mine[None], (cols, share, SIZE)), "col")
+    mine = (jnp.sum(mine.astype(F32) * same[:, None, None], axis=0) * scale).astype(BF16)
     mine, full_grad, half_grad = lax.optimization_barrier((mine, full_grad, half_grad))
-    mine = mine.reshape(lines, SIZE)
-    probe_grad = swap(jnp.broadcast_to(mine[None], (rows, lines, SIZE)), "row")
-    probe_grad = probe_grad.astype(F32).reshape(probe.shape)
+    mine = swap(jnp.broadcast_to(mine[None], (cols, share, SIZE)), "col").reshape(half_probe)
+    given = lax.ppermute(mine, both, partner)
+    even = odd[0] == 0
+    probe_grad = [jnp.where(even, mine, given), jnp.where(even, given, mine)]
+    probe_grad = jnp.concatenate(probe_grad, axis=0).astype(F32)
     half_grad = half_grad.astype(F32)
     nothing = jnp.zeros_like(half_grad)
     odd = odd[0] == 1

time: 166 us -> 162 us (0.976)
  waiting for transfers between devices: 55.9 us -> 45.4 us
  Pallas kernels: 34.3 us -> 44.7 us
  starting transfers between devices: 58.5 us -> 54.8 us
  local copies, waits for them, and re-layouts: 7.2 us -> 5.41 us
    all_to_all x4 -> x3, waiting for transfers between devices: 34.8 us -> 20 us  [swap(): return lax.all_to_all(blocks, axis, split_axis=0, concat_axis=0, tiled=True)]
    ppermute x1, waiting for transfers between devices: 0.49 us -> 6.86 us  [body(): half_grad = lax.ppermute(half_grad, both, ring(-1))]
    all_to_all x4 -> x3, starting transfers between devices: 31.1 us -> 25.4 us  [swap(): return lax.all_to_all(blocks, axis, split_axis=0, concat_axis=0, tiled=True)]
    pallas_call x1, Pallas kernels: 12.6 us -> 18.1 us  [body(): pl.pallas_call(backward_kernel, out_shape=[jax.ShapeDtypeStruct(tile_shap...]
    pallas_call x1, Pallas kernels: 9.3 us -> 13.7 us  [body(): pl.pallas_call(forward_kernel, out_shape=[jax.ShapeDtypeStruct((cols,) +...]
    all_to_all x1, waiting for transfers between devices: 17.5 us -> 13.2 us  [body(): lax.all_to_all(slots, 'col', split_axis=0, concat_axis=0, tiled=True)]
    ppermute x1, starting transfers between devices: 5.25 us -> 8.95 us  [body(): half_grad = lax.ppermute(half_grad, both, ring(-1))]
    convert_element_type x1 -> x4, other arithmetic: 0.01 us -> 3.43 us  [the longest x1 1.96 us: body(): mine = (keep.astype(F32) + given.astype(F32)).astype(BF16)]
  transfers between devices with their start and end apart: 10 -> 11, of which waited for: 7 -> 6; matrix products, arithmetic and copies ran while one was open for 5% -> 4% of each run, Pallas kernels for 11% -> 15%
where the time goes in v3:
time: 162 us; the launch traced here: 160 us
  starting transfers between devices  54.8 us (34%)
  waiting for transfers between devices  45.4 us (28%)
  Pallas kernels  44.7 us (28%)
  other arithmetic  7.97 us (5%)
  local copies, waits for them, and re-layouts  5.41 us (3%)
    all_to_all x3, starting transfers between devices, swap(): return lax.all_to_all(blocks, axis, split_axis=0, concat_axis=0, tiled=True)  25.4 us
    all_to_all x3, waiting for transfers between devices, swap(): return lax.all_to_all(blocks, axis, split_axis=0, concat_axis=0, tiled=True)  20 us
    pallas_call x1, Pallas kernels, body(): pl.pallas_call(backward_kernel, out_shape=[jax.ShapeDtypeStruct(tile_shap...  18.1 us
    pallas_call x1, Pallas kernels, body(): pl.pallas_call(forward_kernel, out_shape=[jax.ShapeDtypeStruct((cols,) +...  13.7 us
    all_to_all x1, waiting for transfers between devices, body(): lax.all_to_all(slots, 'col', split_axis=0, concat_axis=0, tiled=True)  13.2 us
    ppermute x1, starting transfers between devices, body(): half_grad = lax.ppermute(half_grad, both, ring(-1))  8.95 us
    ppermute x1, waiting for transfers between devices, body(): half_grad = lax.ppermute(half_grad, both, ring(-1))  6.86 us
    all_to_all x1, starting transfers between devices, body(): lax.all_to_all(notes, 'col', split_axis=0, concat_axis=0, tiled=True)  6.74 us
  transfers between devices with their start and end apart: 11, of which 6 were waited for; matrix products, arithmetic and copies ran while one was open for 4% of the time, Pallas kernels for 15%

profile of v3, /device:TPU:0, one launch (start us, length us, event | category | flops | bytes accessed | tf_op | source)
XLA Modules:
  0.0 159.8 jit_solution(6057588106278603115)
XLA Ops:
  0.7 3.0 %shard_map.116 = (bf16[2,2,512,256]{3,2,1,0:T(8,128)(2,1)}, bf16[2,2,512,128]{3,2,1,0:T(8,128)(2,1)}) custom-call(s32[1]{0:T(128)} %bitcast.odd, f32[2,2,512,256]{3,2,1,0:T(8,128)} %obj.1), custom_call_target="tpu_custom_call" | custom-call | tf_op jit(solution)/shard_map/pallas_call | solution.py:520
  3.6 5.3 %collective-permute-start = (bf16[2,2,512,256]{3,2,1,0:T(8,128)(2,1)}, bf16[2,2,512,256]{3,2,1,0:T(8,128)(2,1)S(1)}, u32[]{:S(2)}, u32[]{:S(2)}) collective-permute-start(bf16[2,2,512,256]{3,2,1,0:T(8,128)(2,1)} %get-tuple-element.19.tile), channel_id=1, source_target_pairs={{0,15},{1,0},{2,1},{3,2},{4,3},{5,4},{6,5},{7,6},{8,7},{9,8},{10,9... | collective-permute-start | bytes 3145736 | tf_op jit(solution)/shard_map/ppermute | solution.py:530
  8.9 0.0 collective-permute-start.1
  8.9 0.1 copy.16
  9.0 0.1 reshape.40
  9.1 0.1 copy.17
  9.2 0.1 reshape.41
  9.9 0.7 pad_add_fusion.info
  10.6 1.6 %shard_map.113 = s32[16,1,8]{2,1,0:T(1,128)} custom-call(s32[26]{0:T(128)} %pad_add_fusion.info), custom_call_target="tpu_custom_call" | custom-call | tf_op jit(solution)/shard_map/pallas_call | solution.py:535
  12.2 6.7 %all-to-all-start = ((s32[16,1,8]{2,1,0:T(1,128)}), s32[16,1,8]{2,1,0:T(1,128)S(1)}, u32[]{:S(2)}, u32[]{:S(2)}) async-start(s32[16,1,8]{2,1,0:T(1,128)} %shard_map.113), calls=%async_computation | async-start | bytes 16384 | tf_op jit(solution)/shard_map/all_to_all | solution.py:542
  19.0 0.1 rev.3
  19.1 0.6 select_maximum_fusion.taps
  19.7 4.0 %shard_map.114.packed = bf16[6,256,256]{2,1,0:T(8,128)(2,1)} custom-call(s32[26]{0:T(128)} %pad_add_fusion.info, f32[6,256,256]{2,1,0:T(8,128)} %measured.1, bf16[2,256,256]{2,1,0:T(8,128)(2,1)} %constant.45.clone.sort), custom_call_target="tpu_custom_call" | custom-call | tf_op jit(solution)/shard_map/pallas_call | solution.py:543
  23.7 3.1 %all-to-all-done.notes = s32[16,1,8]{2,1,0:T(1,128)S(1)} async-done(((s32[16,1,8]{2,1,0:T(1,128)}), s32[16,1,8]{2,1,0:T(1,128)S(1)}, u32[]{:S(2)}, u32[]{:S(2)}) %all-to-all-start) | async-done | bytes 544 | tf_op jit(solution)/shard_map/all_to_all | solution.py:542
  26.9 0.6 copy-done.4
  27.5 4.4 %shard_map.115 = (s32[16]{0:T(128)}, bf16[16,256,256]{2,1,0:T(8,128)(2,1)}) custom-call(s32[1]{0:T(128)} %bitcast.1.me, s32[16,1,8]{2,1,0:T(1,128)} %copy-done.4, bf16[6,256,256]{2,1,0:T(8,128)(2,1)} %shard_map.114.packed), custom_call_target="tpu_custom_call" | custom-call | tf_op jit(solution)/shard_map/pallas_call | solution.py:550
  31.8 6.4 %all-to-all-start.1 = ((bf16[16,256,256]{2,1,0:T(8,128)(2,1)}), bf16[16,256,256]{2,1,0:T(8,128)(2,1)S(1)}, u32[]{:S(2)}, u32[]{:S(2)}) async-start(bf16[16,256,256]{2,1,0:T(8,128)(2,1)} %get-tuple-element.25), calls=%async_computation.1 | async-start | bytes 4194304 | tf_op jit(solution)/shard_map/all_to_all | solution.py:565
  38.3 0.0 collective-permute-done.full
  38.3 1.1 copy-done.9
  39.4 13.7 %shard_map.117 = (f32[16,1024,512]{2,1,0:T(8,128)}, f32[16,1024,512]{2,1,0:T(8,128)}, f32[16,256,256]{2,1,0:T(8,128)}, bf16[16,2,256,512]{3,2,1,0:T(8,128)(2,1)}) custom-call(s32[1]{0:T(128)} %bitcast.odd, s32[16]{0:T(128)} %get-tuple-element.18.codes, bf16[2,2,512,256]{3,2,1,0:T(8,128)(2,1)} %copy-done.9, bf16[2,2,512,256]{3,2,1,0:T(8,128)(2,1)} %get-tuple-element.19.tile, ...), custom_call_target="tpu_custom_call" | custom-call | flops 40000000000 | bytes 10000000 | tf_op jit(solution)/shard_map/pallas_call | solution.py:584
  53.1 13.2 %all-to-all-done.1.slots_all = bf16[16,256,256]{2,1,0:T(8,128)(2,1)S(1)} async-done(((bf16[16,256,256]{2,1,0:T(8,128)(2,1)}), bf16[16,256,256]{2,1,0:T(8,128)(2,1)S(1)}, u32[]{:S(2)}, u32[]{:S(2)}) %all-to-all-start.1) | async-done | bytes 2097184 | tf_op jit(solution)/shard_map/all_to_all | solution.py:565
  66.3 1.3 copy-done
  67.6 18.1 %shard_map.118 = (f32[2,2,512,256]{3,2,1,0:T(8,128)}, bf16[2,2,512,256]{3,2,1,0:T(8,128)(2,1)}, bf16[2,2,512,128]{3,2,1,0:T(8,128)(2,1)}, bf16[2,2,256,256]{3,2,1,0:T(8,128)(2,1)}, bf16[2,2,256,256]{3,2,1,0:T(8,128)(2,1)}) custom-call(s32[1]{0:T(128)} %bitcast.odd, s32[16]{0:T(128)} %get-tuple-element.18.codes, bf16[4,256,256]{2,1,0:T(8,128)(2,1)} %constant.53.dft, ...), custom_call_target="tpu_custom_call" | custom-call | tf_op jit(solution)/shard_map/pallas_call | solution.py:601
  85.7 0.1 collective-permute-start.2
  85.8 2.1 %collective-permute-done.2 = bf16[2,2,256,256]{3,2,1,0:T(8,128)(2,1)S(1)} collective-permute-done((bf16[2,2,256,256]{3,2,1,0:T(8,128)(2,1)}, bf16[2,2,256,256]{3,2,1,0:T(8,128)(2,1)S(1)}, u32[]{:S(2)}, u32[]{:S(2)}) %collective-permute-start.2) | collective-permute-done | bytes 524320 | tf_op jit(solution)/shard_map/ppermute | solution.py:639
  87.9 2.0 %add_convert_fusion = bf16[2,2,256,256]{3,2,1,0:T(8,128)(2,1)} fusion(bf16[2,2,256,256]{3,2,1,0:T(8,128)(2,1)S(1)} %collective-permute-done.2, bf16[2,2,256,256]{3,2,1,0:T(8,128)(2,1)} %get-tuple-element.27), kind=kLoop, calls=%fused_computation.4 | loop fusion | flops 1048576 | bytes 1572864 | tf_op jit(solution)/shard_map/convert_element_type | solution.py:640
  89.9 9.1 %all-to-all-start.2 = ((bf16[16,64,256]{2,1,0:T(8,128)(2,1)}), bf16[16,64,256]{2,1,0:T(8,128)(2,1)S(1)}, u32[]{:S(2)}, u32[]{:S(2)}) async-start(bf16[16,64,256]{2,1,0:T(8,128)(2,1)} %bitcast.3), calls=%async_computation.2 | async-start | bytes 1048576 | tf_op jit(solution)/shard_map/all_to_all | solution.py:637
  98.9 1.9 %collective-permute-start.3 = (bf16[2,2,512,256]{3,2,1,0:T(8,128)(2,1)}, bf16[2,2,512,256]{3,2,1,0:T(8,128)(2,1)S(1)}, u32[]{:S(2)}, u32[]{:S(2)}) collective-permute-start(bf16[2,2,512,256]{3,2,1,0:T(8,128)(2,1)} %get-tuple-element.29), channel_id=1, source_target_pairs={{0,1},{1,2},{2,3},{3,4},{4,5},{5,6},{6,7},{7,8},{8,9},{9,10},{10,1... | collective-permute-start | bytes 3145736 | tf_op jit(solution)/shard_map/ppermute | solution.py:631
  100.9 9.9 %all-to-all-done.2 = bf16[16,64,256]{2,1,0:T(8,128)(2,1)S(1)} async-done(((bf16[16,64,256]{2,1,0:T(8,128)(2,1)}), bf16[16,64,256]{2,1,0:T(8,128)(2,1)S(1)}, u32[]{:S(2)}, u32[]{:S(2)}) %all-to-all-start.2) | async-done | bytes 524320 | tf_op jit(solution)/shard_map/all_to_all | solution.py:637
  110.8 0.1 reduce_sum.21
  110.9 0.7 broadcast_in_dim.6
  111.6 9.1 %all-to-all-start.3 = ((bf16[8,64,256]{2,1,0:T(8,128)(2,1)}), bf16[8,64,256]{2,1,0:T(8,128)(2,1)S(1)}, u32[]{:S(2)}, u32[]{:S(2)}) async-start(bf16[8,64,256]{2,1,0:T(8,128)(2,1)} %broadcast_in_dim.6), calls=%async_computation.3 | async-start | bytes 524288 | tf_op jit(solution)/shard_map/all_to_all | solution.py:637
  120.7 8.9 %collective-permute-start.4 = (bf16[2,2,512,128]{3,2,1,0:T(8,128)(2,1)}, bf16[2,2,512,128]{3,2,1,0:T(8,128)(2,1)}, u32[]{:S(2)}, u32[]{:S(2)}) collective-permute-start(bf16[2,2,512,128]{3,2,1,0:T(8,128)(2,1)} %get-tuple-element.30), channel_id=1, source_target_pairs={{0,15},{1,0},{2,1},{3,2},{4,3},{5,4},{6,5},{7,6},{8,7},{9,8},{10,9... | collective-permute-start | bytes 1572872 | tf_op jit(solution)/shard_map/ppermute | solution.py:632
  129.7 0.0 all-to-all-done.3
  129.7 0.1 multiply_reduce_fusion
  129.8 0.0 copy-start.1
  129.8 6.9 %collective-permute-done.4 = bf16[2,2,512,128]{3,2,1,0:T(8,128)(2,1)} collective-permute-done((bf16[2,2,512,128]{3,2,1,0:T(8,128)(2,1)}, bf16[2,2,512,128]{3,2,1,0:T(8,128)(2,1)}, u32[]{:S(2)}, u32[]{:S(2)}) %collective-permute-start.4) | collective-permute-done | bytes 524320 | tf_op jit(solution)/shard_map/ppermute | solution.py:632
  136.7 0.0 collective-permute-done.3
  136.7 0.9 broadcast_in_dim.8
  137.6 0.2 copy-done.2
  137.8 7.2 %all-to-all-start.4 = ((bf16[16,64,256]{2,1,0:T(8,128)(2,1)}), bf16[16,64,256]{2,1,0:T(8,128)(2,1)S(1)}, u32[]{:S(2)}, u32[]{:S(2)}) async-start(bf16[16,64,256]{2,1,0:T(8,128)(2,1)} %broadcast_in_dim.8), calls=%async_computation.4 | async-start | bytes 1048576 | tf_op jit(solution)/shard_map/all_to_all | solution.py:637
  145.0 10.1 %all-to-all-done.4 = bf16[16,64,256]{2,1,0:T(8,128)(2,1)S(1)} async-done(((bf16[16,64,256]{2,1,0:T(8,128)(2,1)}), bf16[16,64,256]{2,1,0:T(8,128)(2,1)S(1)}, u32[]{:S(2)}, u32[]{:S(2)}) %all-to-all-start.4) | async-done | bytes 524320 | tf_op jit(solution)/shard_map/all_to_all | solution.py:637
  155.1 0.0 collective-permute-start.5
  155.1 1.3 convert_select_fusion.1
  156.4 0.1 copy-done.3
  156.5 1.7 %maximum_add_fusion = f32[2,2,512,256]{3,2,1,0:T(8,128)} fusion(f32[2,2,512,128]{3,2,1,0:T(8,128)S(1)} %get-tuple-element.37, f32[2,2,512,128]{3,2,1,0:T(8,128)S(1)} %get-tuple-element.36, f32[2,2,512,256]{3,2,1,0:T(8,128)S(1)} %copy-done.1, bf16[2,2,512,256]{3,2,1,0:T(8,128)(2,1)S(1)} %copy-done.3), kind=kLoop, calls=%fused_computation | loop fusion | flops 2097152 | bytes 7340032 | tf_op jit(solution)/shard_map/add | solution.py:657
  158.2 0.1 broadcast_select_fusion.1
  158.3 1.5 maximum_convert_fusion
  (19 shorter events, 0.1 us)
Async XLA Ops:
  0.6 8.3 %copy-start.7 = (s32[6,2]{0,1:T(2,128)S(1)}, s32[6,2]{0,1:T(2,128)}, u32[]{:S(2)}) copy-start(s32[6,2]{0,1:T(2,128)} %param.15) | copy-start | bytes 148
  0.6 8.5 %copy-start.8 = (s32[6,2]{0,1:T(2,128)S(1)}, s32[6,2]{0,1:T(2,128)}, u32[]{:S(2)}) copy-start(s32[6,2]{0,1:T(2,128)} %param.16) | copy-start | bytes 148
  0.7 18.3 %copy-start.6 = (f32[2,64]{1,0:T(2,128)S(1)}, f32[2,64]{1,0:T(2,128)}, u32[]{:S(2)}) copy-start(f32[2,64]{1,0:T(2,128)} %param.13) | copy-start | bytes 1540
  0.7 18.3 %copy-start.5 = (f32[2,64]{1,0:T(2,128)S(1)}, f32[2,64]{1,0:T(2,128)}, u32[]{:S(2)}) copy-start(f32[2,64]{1,0:T(2,128)} %param.14) | copy-start | bytes 1540
  3.6 34.7 %collective-permute-start = (bf16[2,2,512,256]{3,2,1,0:T(8,128)(2,1)}, bf16[2,2,512,256]{3,2,1,0:T(8,128)(2,1)S(1)}, u32[]{:S(2)}, u32[]{:S(2)}) collective-permute-start(bf16[2,2,512,256]{3,2,1,0:T(8,128)(2,1)} %get-tuple-element.19.tile), channel_id=1, source_target_pairs={{0,15},{1,0},{2,1},{3,2},{4,3},{5,4},{6,5},{7,6},{8,7},{9,8},{10,9... | collective-permute-start | bytes 3145736 | tf_op jit(solution)/shard_map/ppermute | solution.py:530
  8.9 29.4 %collective-permute-start.1 = (bf16[2,2,512,128]{3,2,1,0:T(8,128)(2,1)}, bf16[2,2,512,128]{3,2,1,0:T(8,128)(2,1)}, u32[]{:S(2)}, u32[]{:S(2)}) collective-permute-start(bf16[2,2,512,128]{3,2,1,0:T(8,128)(2,1)} %get-tuple-element.20), channel_id=1, source_target_pairs={{0,1},{1,2},{2,3},{3,4},{4,5},{5,6},{6,7},{7,8},{8,9},{9,10},{10,1... | collective-permute-start | bytes 1572872 | tf_op jit(solution)/shard_map/ppermute | solution.py:531
  12.2 14.6 %all-to-all-start = ((s32[16,1,8]{2,1,0:T(1,128)}), s32[16,1,8]{2,1,0:T(1,128)S(1)}, u32[]{:S(2)}, u32[]{:S(2)}) async-start(s32[16,1,8]{2,1,0:T(1,128)} %shard_map.113), calls=%async_computation | async-start | bytes 16384 | tf_op jit(solution)/shard_map/all_to_all | solution.py:542
  26.9 0.6 copy-start.4
  31.8 34.4 %all-to-all-start.1 = ((bf16[16,256,256]{2,1,0:T(8,128)(2,1)}), bf16[16,256,256]{2,1,0:T(8,128)(2,1)S(1)}, u32[]{:S(2)}, u32[]{:S(2)}) async-start(bf16[16,256,256]{2,1,0:T(8,128)(2,1)} %get-tuple-element.25), calls=%async_computation.1 | async-start | bytes 4194304 | tf_op jit(solution)/shard_map/all_to_all | solution.py:565
  38.3 1.1 copy-start.9
  66.3 1.3 copy-start
  85.7 2.2 %collective-permute-start.2 = (bf16[2,2,256,256]{3,2,1,0:T(8,128)(2,1)}, bf16[2,2,256,256]{3,2,1,0:T(8,128)(2,1)S(1)}, u32[]{:S(2)}, u32[]{:S(2)}) collective-permute-start(bf16[2,2,256,256]{3,2,1,0:T(8,128)(2,1)} %get-tuple-element.28), channel_id=1, source_target_pairs={{0,16},{1,17},{2,18},{3,19},{4,20},{5,21},{6,22},{7,23},{8,24},{9,... | collective-permute-start | bytes 1572872 | tf_op jit(solution)/shard_map/ppermute | solution.py:639
  89.9 20.9 %all-to-all-start.2 = ((bf16[16,64,256]{2,1,0:T(8,128)(2,1)}), bf16[16,64,256]{2,1,0:T(8,128)(2,1)S(1)}, u32[]{:S(2)}, u32[]{:S(2)}) async-start(bf16[16,64,256]{2,1,0:T(8,128)(2,1)} %bitcast.3), calls=%async_computation.2 | async-start | bytes 1048576 | tf_op jit(solution)/shard_map/all_to_all | solution.py:637
  98.9 37.8 %collective-permute-start.3 = (bf16[2,2,512,256]{3,2,1,0:T(8,128)(2,1)}, bf16[2,2,512,256]{3,2,1,0:T(8,128)(2,1)S(1)}, u32[]{:S(2)}, u32[]{:S(2)}) collective-permute-start(bf16[2,2,512,256]{3,2,1,0:T(8,128)(2,1)} %get-tuple-element.29), channel_id=1, source_target_pairs={{0,1},{1,2},{2,3},{3,4},{4,5},{5,6},{6,7},{7,8},{8,9},{9,10},{10,1... | collective-permute-start | bytes 3145736 | tf_op jit(solution)/shard_map/ppermute | solution.py:631
  111.6 18.1 %all-to-all-start.3 = ((bf16[8,64,256]{2,1,0:T(8,128)(2,1)}), bf16[8,64,256]{2,1,0:T(8,128)(2,1)S(1)}, u32[]{:S(2)}, u32[]{:S(2)}) async-start(bf16[8,64,256]{2,1,0:T(8,128)(2,1)} %broadcast_in_dim.6), calls=%async_computation.3 | async-start | bytes 524288 | tf_op jit(solution)/shard_map/all_to_all | solution.py:637
  120.7 16.0 %collective-permute-start.4 = (bf16[2,2,512,128]{3,2,1,0:T(8,128)(2,1)}, bf16[2,2,512,128]{3,2,1,0:T(8,128)(2,1)}, u32[]{:S(2)}, u32[]{:S(2)}) collective-permute-start(bf16[2,2,512,128]{3,2,1,0:T(8,128)(2,1)} %get-tuple-element.30), channel_id=1, source_target_pairs={{0,15},{1,0},{2,1},{3,2},{4,3},{5,4},{6,5},{7,6},{8,7},{9,8},{10,9... | collective-permute-start | bytes 1572872 | tf_op jit(solution)/shard_map/ppermute | solution.py:632
  129.8 26.6 %copy-start.1 = (f32[2,2,512,256]{3,2,1,0:T(8,128)S(1)}, f32[2,2,512,256]{3,2,1,0:T(8,128)}, u32[]{:S(2)}) copy-start(f32[2,2,512,256]{3,2,1,0:T(8,128)} %get-tuple-element.26) | copy-start | bytes 6291460
  136.7 1.1 copy-start.2
  137.8 17.3 %all-to-all-start.4 = ((bf16[16,64,256]{2,1,0:T(8,128)(2,1)}), bf16[16,64,256]{2,1,0:T(8,128)(2,1)S(1)}, u32[]{:S(2)}, u32[]{:S(2)}) async-start(bf16[16,64,256]{2,1,0:T(8,128)(2,1)} %broadcast_in_dim.8), calls=%async_computation.4 | async-start | bytes 1048576 | tf_op jit(solution)/shard_map/all_to_all | solution.py:637
  155.1 1.4 copy-start.3
  155.1 3.1 %collective-permute-start.5 = (bf16[2,2,256,256]{3,2,1,0:T(8,128)(2,1)S(1)}, bf16[2,2,256,256]{3,2,1,0:T(8,128)(2,1)S(1)}, u32[]{:S(2)}, u32[]{:S(2)}) collective-permute-start(bf16[2,2,256,256]{3,2,1,0:T(8,128)(2,1)S(1)} %bitcast.6), channel_id=1, source_target_pairs={{0,16},{1,17},{2,18},{3,19},{4,20},{5,21},{6,22},{7,23},{8,24},{9,... | collective-permute-start | bytes 1572872 | tf_op jit(solution)/shard_map/ppermute | solution.py:649
